TPU v7x, 32 devices: a whole 2x2x4 slice. The times are simulated.
32 devices in a mesh: lag: 2 (over y), patch: 16 (over z, x, core).
Axes of the slice: x: 2, y: 2, z: 4, core: 2. Of those that a mesh axis runs over, the one named last changes fastest.
Arguments:
- incident: bfloat16 [4, 8192, 128], P(None, 'patch'), may hold values from -6 to 6
- pending: float32 [2, 8192, 128], P('lag', 'patch'), may hold values from -6 to 6
- self_inverse: float32 [64, 128, 128], P('patch'), may hold values from -0.5 to 0.5
- retarded: float32 [2, 16, 56, 128, 128], P('lag', 'patch'), may hold values from -0.1875 to 0.1875
- block_rows: int32 [2, 16, 56], P('lag', 'patch'), may hold values from -1 to 3, as said below
- block_sources: int32 [2, 16, 56], P('lag', 'patch'), may hold values from -1 to 63, as said below
- owner_map: int32 [64], replicated, may hold values from 0 to 63, as said below
Outputs:
- currents: bfloat16 [4, 8192, 128], P(None, 'patch')
- fields_ahead: float32 [2, 8192, 128], P('lag', 'patch')
Inputs may be any that keep to these rules, and one draw needn't show every extreme that they name: `block_sources`: each device's list holds its live entries first and -1 after them; at most 56 live entries, a count that some device reaches in every draw; the live entries of one device name no (row, source) pair twice and, among them, at most one storage block of each patch owner. `block_rows`: -1 exactly where block_sources is -1. `owner_map`: A permutation of the 64 storage blocks; storage block q is owned by patch q // 4.
All inputs are finite; a program needn't handle non-finite values.
Results may differ from a plain program's by a relative error of at most 0.0055.
Values may be sent and summed in bfloat16 or wider, within the bound.
No kernel may reach another device: no remote copies, remote signals or barrier semaphores. Data moves between devices by JAX's collectives and lax.ppermute only.
A program may use at most 64 MiB of HBM per device.

v0:
```python
import jax
import jax.numpy as jnp
from jax import lax
from jax.experimental import pallas as pl
from jax.experimental.pallas import tpu as pltpu
from jax.sharding import PartitionSpec as P

VMEM, HBM, ANY = pltpu.VMEM, pltpu.HBM, pl.ANY
DMA = pltpu.SemaphoreType.DMA
MIB = 1 << 20


def call(kernel, outs, ins, scratch=(), flops=0, nbytes=0, vmem=0, aliases=None):
    out_shape = tuple(space(dims, dtype) for space, dims, dtype in outs)
    out_specs = tuple(pl.BlockSpec(memory_space=space) for space, _, _ in outs)
    run = pl.pallas_call(
        kernel,
        out_shape=out_shape,
        in_specs=[pl.BlockSpec(memory_space=space) for space, _ in ins],
        out_specs=out_specs,
        scratch_shapes=scratch,
        input_output_aliases=aliases or {},
        cost_estimate=pl.CostEstimate(flops=flops, bytes_accessed=nbytes, transcendentals=0),
        compiler_params=pltpu.CompilerParams(vmem_limit_bytes=vmem + 6 * MIB),
    )
    results = run(*(pltpu.with_memory_space_constraint(x, space) for space, x in ins))
    return results if len(outs) > 1 else results[0]


def started(*copies):
    copies = [pltpu.make_async_copy(*copy) for copy in copies]
    for copy in copies:
        copy.start()
    return copies


def request_kernel(per_patch, sources_hbm, owner_hbm, wanted_hbm, wanted, sources, owner_map, sems):
    copies = started(
        (sources_hbm, sources, sems.at[0]),
        (owner_hbm, owner_map, sems.at[1]),
    )
    patch = lax.broadcasted_iota(jnp.int32, wanted.shape, 0)
    for copy in copies:
        copy.wait()

    def entry(j, table):
        source = sources[0, 0, j]
        storage = owner_map[jnp.maximum(source, 0)]
        here = (patch == storage // per_patch) & (source >= 0)
        return jnp.where(here, storage % per_patch, table)

    wanted[...] = lax.fori_loop(
        0, sources.shape[2], entry, jnp.full(wanted.shape, -1, jnp.int32), unroll=8
    )
    started((wanted, wanted_hbm, sems.at[0]))[0].wait()


def panel_kernel(
    per_patch, rows_hbm, sources_hbm, owner_hbm, retarded, high, low_hbm, rows, sources, owner_map, parts, low, sems
):
    size = retarded.shape[-1]
    slots, chunk = parts.shape[:2]
    chunks = retarded.shape[2] // chunk

    def fetch(c):
        part = retarded.at[0, 0, pl.ds(c * chunk, chunk)]
        return pltpu.make_async_copy(part, parts.at[c % slots], sems.at[c % slots])

    lists = started(
        (rows_hbm, rows, sems.at[slots]),
        (sources_hbm, sources, sems.at[slots + 1]),
        (owner_hbm, owner_map, sems.at[slots + 2]),
    )
    for c in range(min(slots, chunks)):
        fetch(c).start()
    high[...] = jnp.zeros_like(high)
    low[...] = jnp.zeros_like(low)
    for copy in lists:
        copy.wait()

    def entry(c, k, carry):
        source = sources[0, 0, c * chunk + k]

        @pl.when(source >= 0)
        def _():
            owner = owner_map[source] // per_patch
            row = pl.multiple_of(rows[0, 0, c * chunk + k] * size, size)
            column = pl.multiple_of(owner * size, size)
            block = parts[c % slots, k]
            rounded = block.astype(high.dtype)
            rest = (block - rounded.astype(jnp.float32)).astype(low.dtype)
            high[pl.ds(row, size), pl.ds(column, size)] = rounded
            low[pl.ds(row, size), pl.ds(column, size)] = rest

        return carry

    for c in range(chunks):
        fetch(c).wait()
        lax.fori_loop(0, chunk, lambda k, carry, c=c: entry(c, k, carry), 0)
        if c + slots < chunks:
            fetch(c + slots).start()
    started((low, low_hbm, sems.at[0]))[0].wait()


def solved(excess, self_inverse):
    blocks, size, _ = self_inverse.shape
    parts = [
        jnp.dot(
            self_inverse[k],
            excess[k * size : (k + 1) * size],
            precision=lax.Precision.HIGHEST,
            preferred_element_type=jnp.float32,
        )
        for k in range(blocks)
    ]
    return jnp.concatenate(parts, axis=0).astype(jnp.bfloat16)


def products(high, low_hbm, arrived, low, sem, parts=1):
    patches, size, columns = arrived.shape
    (copy,) = started((low_hbm, low, sem))
    rows = high.shape[0] // parts
    for part in range(parts):
        here = slice(part * rows, (part + 1) * rows)
        flat = arrived[...].reshape(patches * size, columns)
        fresh = jnp.dot(high[here], flat, preferred_element_type=jnp.float32)
        if part == 0:
            copy.wait()
        yield here, fresh + jnp.dot(low[here], flat, preferred_element_type=jnp.float32)


def first_kernel(incident_hbm, field_hbm, inverse_hbm, after, current, incident, field, inverse, sems):
    del after

    @pl.when(lax.axis_index("lag") == 0)
    def _():
        copies = started(
            (incident_hbm.at[0], incident, sems.at[0]),
            (inverse_hbm, inverse, sems.at[1]),
            (field_hbm, field, sems.at[2]),
        )
        for copy in copies:
            copy.wait()
        current[...] = solved(incident[...].astype(jnp.float32) - field[...], inverse)


def solve_kernel(
    step, high, low_hbm, arrived, field, incident_hbm, inverse_hbm, current, low, incident, inverse, sems
):
    @pl.when(lax.axis_index("lag") == 0)
    def _():
        copies = started(
            (incident_hbm.at[step], incident, sems.at[0]),
            (inverse_hbm, inverse, sems.at[1]),
        )
        ((_, fresh),) = products(high, low_hbm, arrived, low, sems.at[2])
        for copy in copies:
            copy.wait()
        excess = incident[...].astype(jnp.float32) - (field[...] + fresh)
        current[...] = solved(excess, inverse)


def partial_kernel(high, low_hbm, arrived, field, after, partial, low, sem):
    del after

    @pl.when(lax.axis_index("lag") > 0)
    def _():
        ((_, fresh),) = products(high, low_hbm, arrived, low, sem)
        partial[...] = field[...] + fresh


def ahead_kernel(high, low_hbm, arrived, field, ahead_hbm, low, ahead, sems):
    copies = []
    for here, fresh in products(high, low_hbm, arrived, low, sems.at[0], 2):
        ahead[here] = field[here] + fresh
        copies += started((ahead.at[here], ahead_hbm.at[here], sems.at[len(copies) + 1]))
    for copy in copies:
        copy.wait()


def pack_kernel(step, keeps, early, asked, current, *refs):
    outgoing, currents, sems = refs[-3:]
    patches, size, _ = outgoing.shape
    section = lax.axis_index("lag")

    @pl.when(section < keeps if early else section >= keeps)
    def _():
        copies = []
        for q in range(patches):
            block = jnp.max(jnp.maximum(asked[q], 0))
            start = pl.multiple_of(block * size, size)
            copies.append((current.at[pl.ds(start, size)], outgoing.at[q], sems.at[q]))
        copies.append((current, currents.at[step], sems.at[patches]))
        for copy in started(*copies):
            copy.wait()


def shifted(x):
    sections = lax.axis_size("lag")
    return lax.ppermute(x, "lag", [(i, i - 1) for i in range(1, sections)])


def spread(x):
    sections = lax.axis_size("lag")
    section = lax.axis_index("lag")
    received, keeps = x, 1
    while keeps < sections:
        if keeps > 1:
            x = jnp.where(section < keeps // 2, x, received)
        pairs = [(i, i + keeps) for i in range(keeps) if i + keeps < sections]
        received = lax.ppermute(x, "lag", pairs)
        keeps *= 2
    return x, received, max(keeps // 2, 1)


def body(incident, pending, self_inverse, retarded, block_rows, block_sources, owner_map):
    steps, unknowns, columns = incident.shape
    per_patch, size, _ = self_inverse.shape
    listed = retarded.shape[2]
    patches = lax.axis_size("patch")
    bf16, f32 = jnp.bfloat16, jnp.float32
    all_flops = 4 * unknowns * patches * size * columns
    solve_flops = 12 * unknowns * size * columns
    panel_bytes = 4 * unknowns * patches * size
    column = (unknowns, columns)

    column_bytes = 4 * unknowns * columns
    arrived_bytes = 2 * patches * size * columns

    def exchange(x):
        return lax.all_to_all(x, "patch", split_axis=0, concat_axis=0, tiled=True)

    def pack(step, keeps, early, current, filled, after):
        held = [x for x in filled if x is not None]
        aliases = {}
        for out, x in enumerate(filled):
            if x is not None:
                aliases[2 + len(after) + len(aliases)] = out
        return call(
            lambda *refs: pack_kernel(step, keeps, early, *refs),
            [(HBM, (patches, size, columns), bf16), (HBM, incident.shape, bf16)],
            [(VMEM, asked), (VMEM, current)] + [(VMEM, x) for x in after] + [(HBM, x) for x in held],
            [DMA((patches + 1,))],
            aliases=aliases,
        )

    wanted = call(
        lambda *refs: request_kernel(per_patch, *refs),
        [(HBM, (patches, 1, 128), jnp.int32)],
        [(HBM, block_sources), (HBM, owner_map)],
        [
            pltpu.VMEM((patches, 1, 128), jnp.int32),
            pltpu.SMEM(block_sources.shape, jnp.int32),
            pltpu.SMEM(owner_map.shape, jnp.int32),
            DMA((2,)),
        ],
    )
    asked = exchange(wanted)
    solve_scratch = [pltpu.VMEM(column, bf16), pltpu.VMEM(self_inverse.shape, f32), DMA((3,))]
    current = call(
        first_kernel,
        [(VMEM, column, bf16)],
        [(HBM, incident), (HBM, pending[0]), (HBM, self_inverse), (HBM, wanted)],
        [solve_scratch[0], pltpu.VMEM(column, f32), *solve_scratch[1:]],
        solve_flops,
    )
    chunk = max(n for n in range(1, 9) if listed % n == 0)
    panel = (unknowns, patches * size)
    high, low = call(
        lambda *refs: panel_kernel(per_patch, *refs),
        [(VMEM, panel, bf16), (HBM, panel, bf16)],
        [(HBM, block_rows), (HBM, block_sources), (HBM, owner_map), (HBM, retarded)],
        [
            pltpu.SMEM(block_rows.shape, jnp.int32),
            pltpu.SMEM(block_sources.shape, jnp.int32),
            pltpu.SMEM(owner_map.shape, jnp.int32),
            pltpu.VMEM((3, chunk, size, size), f32),
            pltpu.VMEM(panel, bf16),
            DMA((6,)),
        ],
        nbytes=listed * size * size * 4 + panel_bytes,
        vmem=panel_bytes // 2,
    )

    field = pending[0]
    currents = None
    after = []
    for step in range(steps):
        own, received, keeps = spread(current)
        outgoing, currents = pack(step, keeps, True, own, (None, currents), [])
        if lax.axis_size("lag") > 1:
            outgoing, currents = pack(step, keeps, False, received, (outgoing, currents), after)
        arrived = exchange(outgoing)
        field = shifted(field)
        if step + 1 < steps:
            current = call(
                lambda *refs, n=step + 1: solve_kernel(n, *refs),
                [(VMEM, column, bf16)],
                [
                    (VMEM, high),
                    (HBM, low),
                    (VMEM, arrived),
                    (VMEM, field),
                    (HBM, incident),
                    (HBM, self_inverse),
                ],
                [pltpu.VMEM(panel, bf16), *solve_scratch],
                all_flops + solve_flops,
                panel_bytes + arrived_bytes,
                panel_bytes + arrived_bytes,
            )
            field = call(
                partial_kernel,
                [(VMEM, column, f32)],
                [(VMEM, high), (HBM, low), (VMEM, arrived), (VMEM, field), (VMEM, current)],
                [pltpu.VMEM(panel, bf16), DMA],
                all_flops,
                panel_bytes + arrived_bytes,
                panel_bytes + arrived_bytes,
            )
            after = [field]
        else:
            field = call(
                ahead_kernel,
                [(HBM, column, f32)],
                [(VMEM, high), (HBM, low), (VMEM, arrived), (VMEM, field)],
                [pltpu.VMEM(panel, bf16), pltpu.VMEM(column, f32), DMA((3,))],
                all_flops,
                panel_bytes + arrived_bytes,
                panel_bytes + arrived_bytes,
            )
    return currents, field[None]


def solution(mesh):
    in_specs = (
        P(None, "patch", None),
        P("lag", "patch", None),
        P("patch", None, None),
        P("lag", "patch", None, None, None),
        P("lag", "patch", None),
        P("lag", "patch", None),
        P(),
    )
    out_specs = (P(None, "patch", None), P("lag", "patch", None))
    return jax.shard_map(body, mesh=mesh, in_specs=in_specs, out_specs=out_specs, check_vma=False)
```

profile of v0, /device:TPU:0, one launch (start us, length us, event | category | flops | bytes accessed | tf_op | source)
XLA Modules:
  0.0 124.5 jit_solution(13354167908955018794)
XLA Ops:
  0.6 1.9 %shard_map.86.after = s32[16,1,128]{2,1,0:T(1,128)} custom-call(s32[1,1,56]{2,1,0:T(1,128)} %refs_1_.3, s32[64]{0:T(128)} %refs_2_.1), custom_call_target="tpu_custom_call" | custom-call | tf_op jit(solution)/shard_map/pallas_call | solution.py:26
  2.6 1.5 %shard_map.88.refs_1_ = bf16[512,128]{1,0:T(8,128)(2,1)S(1)} custom-call(bf16[4,512,128]{2,1,0:T(8,128)(2,1)} %refs_4_.5, f32[512,128]{1,0:T(8,128)} %bitcast.3, f32[4,128,128]{2,1,0:T(8,128)} %refs_5_.5, s32[16,1,128]{2,1,0:T(1,128)} %shard_map.86.after), custom_call_target="tpu_custom_call" | custom-call | flops 100663296 | tf_op jit(solution)/shard_map/pallas_call | solution.py:26
  4.1 3.4 %collective-permute-start = (bf16[512,128]{1,0:T(8,128)(2,1)S(1)}, bf16[512,128]{1,0:T(8,128)(2,1)S(1)}, u32[]{:S(2)}, u32[]{:S(2)}) collective-permute-start(bf16[512,128]{1,0:T(8,128)(2,1)S(1)} %shard_map.88.refs_1_), channel_id=1, source_target_pairs={{0,16},{1,17},{2,18},{3,19},{4,20},{5,21},{6,22},{7,23},{8,24},{9,... | collective-permute-start | bytes 393224 | tf_op jit(solution)/shard_map/ppermute | solution.py:211
  7.5 12.3 %all_to_all.25.refs_0_ = s32[16,1,128]{2,1,0:T(1,128)S(1)} all-to-all(s32[16,1,128]{2,1,0:T(1,128)} %shard_map.86.after), channel_id=1, replica_groups=mesh['lag'=2,'patch'=16] {'patch'}, dimensions={0} | all-to-all | bytes 16384 | tf_op jit(solution)/shard_map/all_to_all | solution.py:231
  21.1 3.6 %all-to-all-start.1 = ((bf16[16,128,128]{2,1,0:T(8,128)(2,1)}), bf16[16,128,128]{2,1,0:T(8,128)(2,1)S(1)}, u32[]{:S(2)}, u32[]{:S(2)}) async-start(bf16[16,128,128]{2,1,0:T(8,128)(2,1)} %get-tuple-element.24), calls=%async_computation.1 | async-start | bytes 1048576 | tf_op jit(solution)/shard_map/all_to_all | solution.py:231
  24.7 1.3 %collective-permute-start.1 = (f32[512,128]{1,0:T(8,128)S(1)}, f32[512,128]{1,0:T(8,128)S(1)}, u32[]{:S(2)}, u32[]{:S(2)}) collective-permute-start(f32[512,128]{1,0:T(8,128)S(1)} %bitcast.4), channel_id=1, source_target_pairs={{16,0},{17,1},{18,2},{19,3},{20,4},{21,5},{22,6},{23,7},{24,8},{25... | collective-permute-start | bytes 786440 | tf_op jit(solution)/shard_map/ppermute | solution.py:200
  26.0 5.3 %shard_map.87 = (bf16[512,2048]{1,0:T(8,128)(2,1)S(1)}, bf16[512,2048]{1,0:T(8,128)(2,1)}) custom-call(s32[1,1,56]{2,1,0:T(1,128)} %refs_0_.3, s32[1,1,56]{2,1,0:T(1,128)} %refs_1_.3, s32[64]{0:T(128)} %refs_2_.1, f32[1,1,56,128,128]{4,3,2,1,0:T(8,128)} %refs_3_.1), custom_call_target="tpu_custom_call" | custom-call | bytes 7864320 | tf_op jit(solution)/shard_map/pallas_call | solution.py:26
  31.3 3.8 %collective-permute-done.1.refs_3_.field = f32[512,128]{1,0:T(8,128)S(1)} collective-permute-done((f32[512,128]{1,0:T(8,128)S(1)}, f32[512,128]{1,0:T(8,128)S(1)}, u32[]{:S(2)}, u32[]{:S(2)}) %collective-permute-start.1) | collective-permute-done | bytes 262176 | tf_op jit(solution)/shard_map/ppermute | solution.py:200
  35.1 4.0 %all-to-all-done.1.refs_2_.arrived = bf16[16,128,128]{2,1,0:T(8,128)(2,1)S(1)} async-done(((bf16[16,128,128]{2,1,0:T(8,128)(2,1)}), bf16[16,128,128]{2,1,0:T(8,128)(2,1)S(1)}, u32[]{:S(2)}, u32[]{:S(2)}) %all-to-all-start.1) | async-done | bytes 524320 | tf_op jit(solution)/shard_map/all_to_all | solution.py:231
  39.2 3.4 %shard_map.91.after.refs_1_ = bf16[512,128]{1,0:T(8,128)(2,1)S(1)} custom-call(bf16[512,2048]{1,0:T(8,128)(2,1)S(1)} %get-tuple-element.20.refs_0_.high, bf16[512,2048]{1,0:T(8,128)(2,1)} %get-tuple-element.21.refs_1_.low_hbm, bf16[16,128,128]{2,1,0:T(8,128)(2,1)S(1)} %all-to-all-done.1.refs_2_.arrived, f32[512,128]{1,0:T(8,128)S(1)} %collective-permute-done.1.refs_3_.field, ...), custom_call_target="tpu_custom_call" | custom-call | flops 637534208 | bytes 4718592 | tf_op jit(solution)/shard_map/pallas_call | solution.py:26
  42.6 1.3 %collective-permute-start.2 = (bf16[512,128]{1,0:T(8,128)(2,1)S(1)}, bf16[512,128]{1,0:T(8,128)(2,1)S(1)}, u32[]{:S(2)}, u32[]{:S(2)}) collective-permute-start(bf16[512,128]{1,0:T(8,128)(2,1)S(1)} %shard_map.91.after.refs_1_), channel_id=1, source_target_pairs={{0,16},{1,17},{2,18},{3,19},{4,20},{5,21},{6,22},{7,23},{8,24},{9,... | collective-permute-start | bytes 393224 | tf_op jit(solution)/shard_map/ppermute | solution.py:211
  43.9 1.2 shard_map.93
  45.1 2.0 %collective-permute-done.2.refs_1_ = bf16[512,128]{1,0:T(8,128)(2,1)S(1)} collective-permute-done((bf16[512,128]{1,0:T(8,128)(2,1)S(1)}, bf16[512,128]{1,0:T(8,128)(2,1)S(1)}, u32[]{:S(2)}, u32[]{:S(2)}) %collective-permute-start.2) | collective-permute-done | bytes 131104 | tf_op jit(solution)/shard_map/ppermute | solution.py:211
  47.3 4.3 %all-to-all-start.2 = ((bf16[16,128,128]{2,1,0:T(8,128)(2,1)}), bf16[16,128,128]{2,1,0:T(8,128)(2,1)S(1)}, u32[]{:S(2)}, u32[]{:S(2)}) async-start(bf16[16,128,128]{2,1,0:T(8,128)(2,1)} %get-tuple-element.28), calls=%async_computation.2 | async-start | bytes 1048576 | tf_op jit(solution)/shard_map/all_to_all | solution.py:231
  51.6 1.3 %collective-permute-start.3 = (f32[512,128]{1,0:T(8,128)S(1)}, f32[512,128]{1,0:T(8,128)S(1)}, u32[]{:S(2)}, u32[]{:S(2)}) collective-permute-start(f32[512,128]{1,0:T(8,128)S(1)} %shard_map.92.refs_2_), channel_id=1, source_target_pairs={{16,0},{17,1},{18,2},{19,3},{20,4},{21,5},{22,6},{23,7},{24,8},{25... | collective-permute-start | bytes 786440 | tf_op jit(solution)/shard_map/ppermute | solution.py:200
  52.9 10.3 %collective-permute-done.3.refs_3_.field = f32[512,128]{1,0:T(8,128)S(1)} collective-permute-done((f32[512,128]{1,0:T(8,128)S(1)}, f32[512,128]{1,0:T(8,128)S(1)}, u32[]{:S(2)}, u32[]{:S(2)}) %collective-permute-start.3) | collective-permute-done | bytes 262176 | tf_op jit(solution)/shard_map/ppermute | solution.py:200
  63.2 2.8 %all-to-all-done.2.refs_2_.arrived = bf16[16,128,128]{2,1,0:T(8,128)(2,1)S(1)} async-done(((bf16[16,128,128]{2,1,0:T(8,128)(2,1)}), bf16[16,128,128]{2,1,0:T(8,128)(2,1)S(1)}, u32[]{:S(2)}, u32[]{:S(2)}) %all-to-all-start.2) | async-done | bytes 524320 | tf_op jit(solution)/shard_map/all_to_all | solution.py:231
  66.0 3.4 %shard_map.95.after.refs_1_ = bf16[512,128]{1,0:T(8,128)(2,1)S(1)} custom-call(bf16[512,2048]{1,0:T(8,128)(2,1)S(1)} %get-tuple-element.20.refs_0_.high, bf16[512,2048]{1,0:T(8,128)(2,1)} %get-tuple-element.21.refs_1_.low_hbm, bf16[16,128,128]{2,1,0:T(8,128)(2,1)S(1)} %all-to-all-done.2.refs_2_.arrived, f32[512,128]{1,0:T(8,128)S(1)} %collective-permute-done.3.refs_3_.field, ...), custom_call_target="tpu_custom_call" | custom-call | flops 637534208 | bytes 4718592 | tf_op jit(solution)/shard_map/pallas_call | solution.py:26
  69.5 2.0 %collective-permute-start.4 = (bf16[512,128]{1,0:T(8,128)(2,1)S(1)}, bf16[512,128]{1,0:T(8,128)(2,1)S(1)}, u32[]{:S(2)}, u32[]{:S(2)}) collective-permute-start(bf16[512,128]{1,0:T(8,128)(2,1)S(1)} %shard_map.95.after.refs_1_), channel_id=1, source_target_pairs={{0,16},{1,17},{2,18},{3,19},{4,20},{5,21},{6,22},{7,23},{8,24},{9,... | collective-permute-start | bytes 393224 | tf_op jit(solution)/shard_map/ppermute | solution.py:211
  72.7 1.7 %collective-permute-done.4.refs_1_ = bf16[512,128]{1,0:T(8,128)(2,1)S(1)} collective-permute-done((bf16[512,128]{1,0:T(8,128)(2,1)S(1)}, bf16[512,128]{1,0:T(8,128)(2,1)S(1)}, u32[]{:S(2)}, u32[]{:S(2)}) %collective-permute-start.4) | collective-permute-done | bytes 131104 | tf_op jit(solution)/shard_map/ppermute | solution.py:211
  74.6 4.4 %all-to-all-start.3 = ((bf16[16,128,128]{2,1,0:T(8,128)(2,1)}), bf16[16,128,128]{2,1,0:T(8,128)(2,1)S(1)}, u32[]{:S(2)}, u32[]{:S(2)}) async-start(bf16[16,128,128]{2,1,0:T(8,128)(2,1)} %get-tuple-element.32), calls=%async_computation.3 | async-start | bytes 1048576 | tf_op jit(solution)/shard_map/all_to_all | solution.py:231
  79.0 1.3 %collective-permute-start.5 = (f32[512,128]{1,0:T(8,128)S(1)}, f32[512,128]{1,0:T(8,128)S(1)}, u32[]{:S(2)}, u32[]{:S(2)}) collective-permute-start(f32[512,128]{1,0:T(8,128)S(1)} %shard_map.96.refs_2_), channel_id=1, source_target_pairs={{16,0},{17,1},{18,2},{19,3},{20,4},{21,5},{22,6},{23,7},{24,8},{25... | collective-permute-start | bytes 786440 | tf_op jit(solution)/shard_map/ppermute | solution.py:200
  80.3 10.3 %collective-permute-done.5.refs_3_.field = f32[512,128]{1,0:T(8,128)S(1)} collective-permute-done((f32[512,128]{1,0:T(8,128)S(1)}, f32[512,128]{1,0:T(8,128)S(1)}, u32[]{:S(2)}, u32[]{:S(2)}) %collective-permute-start.5) | collective-permute-done | bytes 262176 | tf_op jit(solution)/shard_map/ppermute | solution.py:200
  90.6 2.8 %all-to-all-done.3.refs_2_.arrived = bf16[16,128,128]{2,1,0:T(8,128)(2,1)S(1)} async-done(((bf16[16,128,128]{2,1,0:T(8,128)(2,1)}), bf16[16,128,128]{2,1,0:T(8,128)(2,1)S(1)}, u32[]{:S(2)}, u32[]{:S(2)}) %all-to-all-start.3) | async-done | bytes 524320 | tf_op jit(solution)/shard_map/all_to_all | solution.py:231
  93.4 3.4 %shard_map.99.after.refs_1_ = bf16[512,128]{1,0:T(8,128)(2,1)S(1)} custom-call(bf16[512,2048]{1,0:T(8,128)(2,1)S(1)} %get-tuple-element.20.refs_0_.high, bf16[512,2048]{1,0:T(8,128)(2,1)} %get-tuple-element.21.refs_1_.low_hbm, bf16[16,128,128]{2,1,0:T(8,128)(2,1)S(1)} %all-to-all-done.3.refs_2_.arrived, f32[512,128]{1,0:T(8,128)S(1)} %collective-permute-done.5.refs_3_.field, ...), custom_call_target="tpu_custom_call" | custom-call | flops 637534208 | bytes 4718592 | tf_op jit(solution)/shard_map/pallas_call | solution.py:26
  96.9 2.0 %collective-permute-start.6 = (bf16[512,128]{1,0:T(8,128)(2,1)S(1)}, bf16[512,128]{1,0:T(8,128)(2,1)S(1)}, u32[]{:S(2)}, u32[]{:S(2)}) collective-permute-start(bf16[512,128]{1,0:T(8,128)(2,1)S(1)} %shard_map.99.after.refs_1_), channel_id=1, source_target_pairs={{0,16},{1,17},{2,18},{3,19},{4,20},{5,21},{6,22},{7,23},{8,24},{9,... | collective-permute-start | bytes 393224 | tf_op jit(solution)/shard_map/ppermute | solution.py:211
  100.3 1.5 %collective-permute-done.6.refs_1_ = bf16[512,128]{1,0:T(8,128)(2,1)S(1)} collective-permute-done((bf16[512,128]{1,0:T(8,128)(2,1)S(1)}, bf16[512,128]{1,0:T(8,128)(2,1)S(1)}, u32[]{:S(2)}, u32[]{:S(2)}) %collective-permute-start.6) | collective-permute-done | bytes 131104 | tf_op jit(solution)/shard_map/ppermute | solution.py:211
  102.0 4.4 %all-to-all-start.4 = ((bf16[16,128,128]{2,1,0:T(8,128)(2,1)}), bf16[16,128,128]{2,1,0:T(8,128)(2,1)S(1)}, u32[]{:S(2)}, u32[]{:S(2)}) async-start(bf16[16,128,128]{2,1,0:T(8,128)(2,1)} %get-tuple-element.37), calls=%async_computation.4 | async-start | bytes 1048576 | tf_op jit(solution)/shard_map/all_to_all | solution.py:231
  106.4 1.3 %collective-permute-start.7 = (f32[512,128]{1,0:T(8,128)S(1)}, f32[512,128]{1,0:T(8,128)S(1)}, u32[]{:S(2)}, u32[]{:S(2)}) collective-permute-start(f32[512,128]{1,0:T(8,128)S(1)} %shard_map.100.refs_2_), channel_id=1, source_target_pairs={{16,0},{17,1},{18,2},{19,3},{20,4},{21,5},{22,6},{23,7},{24,8},{25... | collective-permute-start | bytes 786440 | tf_op jit(solution)/shard_map/ppermute | solution.py:200
  107.7 10.3 %collective-permute-done.7.field = f32[512,128]{1,0:T(8,128)S(1)} collective-permute-done((f32[512,128]{1,0:T(8,128)S(1)}, f32[512,128]{1,0:T(8,128)S(1)}, u32[]{:S(2)}, u32[]{:S(2)}) %collective-permute-start.7) | collective-permute-done | bytes 262176 | tf_op jit(solution)/shard_map/ppermute | solution.py:200
  118.0 2.8 %all-to-all-done.4.arrived = bf16[16,128,128]{2,1,0:T(8,128)(2,1)S(1)} async-done(((bf16[16,128,128]{2,1,0:T(8,128)(2,1)}), bf16[16,128,128]{2,1,0:T(8,128)(2,1)S(1)}, u32[]{:S(2)}, u32[]{:S(2)}) %all-to-all-start.4) | async-done | bytes 524320 | tf_op jit(solution)/shard_map/all_to_all | solution.py:231
  120.8 3.5 %shard_map.103 = f32[512,128]{1,0:T(8,128)} custom-call(bf16[512,2048]{1,0:T(8,128)(2,1)S(1)} %get-tuple-element.20.refs_0_.high, bf16[512,2048]{1,0:T(8,128)(2,1)} %get-tuple-element.21.refs_1_.low_hbm, bf16[16,128,128]{2,1,0:T(8,128)(2,1)S(1)} %all-to-all-done.4.arrived, f32[512,128]{1,0:T(8,128)S(1)} %collective-permute-done.7.field), custom_call_target="tpu_custom_call" | custom-call | flops 536870912 | bytes 4718592 | tf_op jit(solution)/shard_map/pallas_call | solution.py:26
  (13 shorter events, 4.5 us)
Async XLA Ops:
  0.6 24.1 %copy-start = (f32[1,512,128]{2,1,0:T(8,128)S(1)}, f32[1,512,128]{2,1,0:T(8,128)}, u32[]{:S(2)}) copy-start(f32[1,512,128]{2,1,0:T(8,128)} %param.8) | copy-start | bytes 786436
  4.1 16.9 %collective-permute-start = (bf16[512,128]{1,0:T(8,128)(2,1)S(1)}, bf16[512,128]{1,0:T(8,128)(2,1)S(1)}, u32[]{:S(2)}, u32[]{:S(2)}) collective-permute-start(bf16[512,128]{1,0:T(8,128)(2,1)S(1)} %shard_map.88.refs_1_), channel_id=1, source_target_pairs={{0,16},{1,17},{2,18},{3,19},{4,20},{5,21},{6,22},{7,23},{8,24},{9,... | collective-permute-start | bytes 393224 | tf_op jit(solution)/shard_map/ppermute | solution.py:211
  21.1 18.0 %all-to-all-start.1 = ((bf16[16,128,128]{2,1,0:T(8,128)(2,1)}), bf16[16,128,128]{2,1,0:T(8,128)(2,1)S(1)}, u32[]{:S(2)}, u32[]{:S(2)}) async-start(bf16[16,128,128]{2,1,0:T(8,128)(2,1)} %get-tuple-element.24), calls=%async_computation.1 | async-start | bytes 1048576 | tf_op jit(solution)/shard_map/all_to_all | solution.py:231
  24.7 10.4 %collective-permute-start.1 = (f32[512,128]{1,0:T(8,128)S(1)}, f32[512,128]{1,0:T(8,128)S(1)}, u32[]{:S(2)}, u32[]{:S(2)}) collective-permute-start(f32[512,128]{1,0:T(8,128)S(1)} %bitcast.4), channel_id=1, source_target_pairs={{16,0},{17,1},{18,2},{19,3},{20,4},{21,5},{22,6},{23,7},{24,8},{25... | collective-permute-start | bytes 786440 | tf_op jit(solution)/shard_map/ppermute | solution.py:200
  42.6 4.5 %collective-permute-start.2 = (bf16[512,128]{1,0:T(8,128)(2,1)S(1)}, bf16[512,128]{1,0:T(8,128)(2,1)S(1)}, u32[]{:S(2)}, u32[]{:S(2)}) collective-permute-start(bf16[512,128]{1,0:T(8,128)(2,1)S(1)} %shard_map.91.after.refs_1_), channel_id=1, source_target_pairs={{0,16},{1,17},{2,18},{3,19},{4,20},{5,21},{6,22},{7,23},{8,24},{9,... | collective-permute-start | bytes 393224 | tf_op jit(solution)/shard_map/ppermute | solution.py:211
  47.3 18.8 %all-to-all-start.2 = ((bf16[16,128,128]{2,1,0:T(8,128)(2,1)}), bf16[16,128,128]{2,1,0:T(8,128)(2,1)S(1)}, u32[]{:S(2)}, u32[]{:S(2)}) async-start(bf16[16,128,128]{2,1,0:T(8,128)(2,1)} %get-tuple-element.28), calls=%async_computation.2 | async-start | bytes 1048576 | tf_op jit(solution)/shard_map/all_to_all | solution.py:231
  51.6 11.6 %collective-permute-start.3 = (f32[512,128]{1,0:T(8,128)S(1)}, f32[512,128]{1,0:T(8,128)S(1)}, u32[]{:S(2)}, u32[]{:S(2)}) collective-permute-start(f32[512,128]{1,0:T(8,128)S(1)} %shard_map.92.refs_2_), channel_id=1, source_target_pairs={{16,0},{17,1},{18,2},{19,3},{20,4},{21,5},{22,6},{23,7},{24,8},{25... | collective-permute-start | bytes 786440 | tf_op jit(solution)/shard_map/ppermute | solution.py:200
  69.5 4.9 %collective-permute-start.4 = (bf16[512,128]{1,0:T(8,128)(2,1)S(1)}, bf16[512,128]{1,0:T(8,128)(2,1)S(1)}, u32[]{:S(2)}, u32[]{:S(2)}) collective-permute-start(bf16[512,128]{1,0:T(8,128)(2,1)S(1)} %shard_map.95.after.refs_1_), channel_id=1, source_target_pairs={{0,16},{1,17},{2,18},{3,19},{4,20},{5,21},{6,22},{7,23},{8,24},{9,... | collective-permute-start | bytes 393224 | tf_op jit(solution)/shard_map/ppermute | solution.py:211
  74.6 18.9 %all-to-all-start.3 = ((bf16[16,128,128]{2,1,0:T(8,128)(2,1)}), bf16[16,128,128]{2,1,0:T(8,128)(2,1)S(1)}, u32[]{:S(2)}, u32[]{:S(2)}) async-start(bf16[16,128,128]{2,1,0:T(8,128)(2,1)} %get-tuple-element.32), calls=%async_computation.3 | async-start | bytes 1048576 | tf_op jit(solution)/shard_map/all_to_all | solution.py:231
  79.0 11.6 %collective-permute-start.5 = (f32[512,128]{1,0:T(8,128)S(1)}, f32[512,128]{1,0:T(8,128)S(1)}, u32[]{:S(2)}, u32[]{:S(2)}) collective-permute-start(f32[512,128]{1,0:T(8,128)S(1)} %shard_map.96.refs_2_), channel_id=1, source_target_pairs={{16,0},{17,1},{18,2},{19,3},{20,4},{21,5},{22,6},{23,7},{24,8},{25... | collective-permute-start | bytes 786440 | tf_op jit(solution)/shard_map/ppermute | solution.py:200
  96.9 4.9 %collective-permute-start.6 = (bf16[512,128]{1,0:T(8,128)(2,1)S(1)}, bf16[512,128]{1,0:T(8,128)(2,1)S(1)}, u32[]{:S(2)}, u32[]{:S(2)}) collective-permute-start(bf16[512,128]{1,0:T(8,128)(2,1)S(1)} %shard_map.99.after.refs_1_), channel_id=1, source_target_pairs={{0,16},{1,17},{2,18},{3,19},{4,20},{5,21},{6,22},{7,23},{8,24},{9,... | collective-permute-start | bytes 393224 | tf_op jit(solution)/shard_map/ppermute | solution.py:211
  102.0 18.9 %all-to-all-start.4 = ((bf16[16,128,128]{2,1,0:T(8,128)(2,1)}), bf16[16,128,128]{2,1,0:T(8,128)(2,1)S(1)}, u32[]{:S(2)}, u32[]{:S(2)}) async-start(bf16[16,128,128]{2,1,0:T(8,128)(2,1)} %get-tuple-element.37), calls=%async_computation.4 | async-start | bytes 1048576 | tf_op jit(solution)/shard_map/all_to_all | solution.py:231
  106.4 11.6 %collective-permute-start.7 = (f32[512,128]{1,0:T(8,128)S(1)}, f32[512,128]{1,0:T(8,128)S(1)}, u32[]{:S(2)}, u32[]{:S(2)}) collective-permute-start(f32[512,128]{1,0:T(8,128)S(1)} %shard_map.100.refs_2_), channel_id=1, source_target_pairs={{16,0},{17,1},{18,2},{19,3},{20,4},{21,5},{22,6},{23,7},{24,8},{25... | collective-permute-start | bytes 786440 | tf_op jit(solution)/shard_map/ppermute | solution.py:200
where the time goes:
time: 126 us; the launch traced here: 125 us
  waiting for transfers between devices  52.5 us (42%)
  starting transfers between devices  30.6 us (24%)
  Pallas kernels  28.2 us (22%)
  blocking collectives  12.3 us (10%)
    ppermute x4, waiting for transfers between devices, shifted(): return lax.ppermute(x, 'lag', [(i, i - 1) for i in range(1, sections)])  34.9 us
    pallas_call x18, Pallas kernels, call(): run(*(pltpu.with_memory_space_constraint(x, space) for space, x in ins))  28.2 us
    all_to_all x4, starting transfers between devices, exchange(): return lax.all_to_all(x, 'patch', split_axis=0, concat_axis=0, tiled=True)  16.7 us
    all_to_all x4, waiting for transfers between devices, exchange(): return lax.all_to_all(x, 'patch', split_axis=0, concat_axis=0, tiled=True)  12.5 us
    all_to_all x1, blocking collectives, exchange(): return lax.all_to_all(x, 'patch', split_axis=0, concat_axis=0, tiled=True)  12.3 us
    ppermute x4, starting transfers between devices, spread(): received = lax.ppermute(x, 'lag', pairs)  8.72 us
    ppermute x4, starting transfers between devices, shifted(): return lax.ppermute(x, 'lag', [(i, i - 1) for i in range(1, sections)])  5.17 us
    ppermute x4, waiting for transfers between devices, spread(): received = lax.ppermute(x, 'lag', pairs)  5.13 us
  transfers between devices with their start and end apart: 12, of which 11 were waited for; matrix products, arithmetic and copies ran while one was open for 0% of the time, Pallas kernels for 8%

commit v1 on v0

--- a/solution.py
+++ b/solution.py
@@ -160,39 +160,51 @@
         current[...] = solved(excess, inverse)
 
 
-def partial_kernel(high, low_hbm, arrived, field, after, partial, low, sem):
-    del after
-
+def partial_kernel(high, low_hbm, arrived, field, partial, low, sem):
     @pl.when(lax.axis_index("lag") > 0)
     def _():
         ((_, fresh),) = products(high, low_hbm, arrived, low, sem)
         partial[...] = field[...] + fresh
 
 
-def ahead_kernel(high, low_hbm, arrived, field, ahead_hbm, low, ahead, sems):
+def ahead_kernel(high, low_hbm, arrived_first, arrived_rest, field, ahead_hbm, low, ahead, sems):
+    def finish(arrived):
+        copies = []
+        for here, fresh in products(high, low_hbm, arrived, low, sems.at[0], 2):
+            ahead[here] = field[here] + fresh
+            copies += started((ahead.at[here], ahead_hbm.at[here], sems.at[len(copies) + 1]))
+        for copy in copies:
+            copy.wait()
+
+    first = lax.axis_index("lag") == 0
+    pl.when(first)(lambda: finish(arrived_first))
+    pl.when(jnp.logical_not(first))(lambda: finish(arrived_rest))
+
+
+def pack(step, asked, current, outgoing, currents, sems):
+    patches, size, _ = outgoing.shape
     copies = []
-    for here, fresh in products(high, low_hbm, arrived, low, sems.at[0], 2):
-        ahead[here] = field[here] + fresh
-        copies += started((ahead.at[here], ahead_hbm.at[here], sems.at[len(copies) + 1]))
-    for copy in copies:
+    for q in range(patches):
+        block = jnp.max(jnp.maximum(asked[q], 0))
+        start = pl.multiple_of(block * size, size)
+        copies.append((current.at[pl.ds(start, size)], outgoing.at[q], sems.at[q]))
+    copies.append((current, currents.at[step], sems.at[patches]))
+    for copy in started(*copies):
         copy.wait()
 
 
-def pack_kernel(step, keeps, early, asked, current, *refs):
+def first_pack_kernel(step, asked, current, *refs):
+    outgoing, currents, _, sems = refs[-4:]
+    pl.when(lax.axis_index("lag") == 0)(lambda: pack(step, asked, current, outgoing, currents, sems))
+
+
+def rest_pack_kernel(step, keeps, asked, own, received, *refs):
     outgoing, currents, sems = refs[-3:]
-    patches, size, _ = outgoing.shape
     section = lax.axis_index("lag")
-
-    @pl.when(section < keeps if early else section >= keeps)
-    def _():
-        copies = []
-        for q in range(patches):
-            block = jnp.max(jnp.maximum(asked[q], 0))
-            start = pl.multiple_of(block * size, size)
-            copies.append((current.at[pl.ds(start, size)], outgoing.at[q], sems.at[q]))
-        copies.append((current, currents.at[step], sems.at[patches]))
-        for copy in started(*copies):
-            copy.wait()
+    if keeps > 1:
+        mine = (section > 0) & (section < keeps)
+        pl.when(mine)(lambda: pack(step, asked, own, outgoing, currents, sems))
+    pl.when(section >= keeps)(lambda: pack(step, asked, received, outgoing, currents, sems))
 
 
 def shifted(x):
@@ -230,18 +242,26 @@
     def exchange(x):
         return lax.all_to_all(x, "patch", split_axis=0, concat_axis=0, tiled=True)
 
-    def pack(step, keeps, early, current, filled, after):
-        held = [x for x in filled if x is not None]
-        aliases = {}
-        for out, x in enumerate(filled):
-            if x is not None:
-                aliases[2 + len(after) + len(aliases)] = out
+    blocks = (patches, size, columns)
+
+    def first_pack(step, current, currents):
+        held = [] if currents is None else [(HBM, currents)]
         return call(
-            lambda *refs: pack_kernel(step, keeps, early, *refs),
-            [(HBM, (patches, size, columns), bf16), (HBM, incident.shape, bf16)],
-            [(VMEM, asked), (VMEM, current)] + [(VMEM, x) for x in after] + [(HBM, x) for x in held],
+            lambda *refs: first_pack_kernel(step, *refs),
+            [(HBM, blocks, bf16), (HBM, incident.shape, bf16), (VMEM, column, bf16)],
+            [(VMEM, asked), (VMEM, current)] + held,
             [DMA((patches + 1,))],
-            aliases=aliases,
+            aliases={1: 2, 2: 1} if held else {1: 2},
+        )
+
+    def rest_pack(step, keeps, own, received, currents, after):
+        ins = [(VMEM, asked), (VMEM, own), (VMEM, received)] + [(VMEM, x) for x in after] + [(HBM, currents)]
+        return call(
+            lambda *refs: rest_pack_kernel(step, keeps, *refs),
+            [(HBM, blocks, bf16), (HBM, incident.shape, bf16)],
+            ins,
+            [DMA((patches + 1,))],
+            aliases={len(ins) - 1: 1},
         )
 
     wanted = call(
@@ -286,11 +306,12 @@
     currents = None
     after = []
     for step in range(steps):
-        own, received, keeps = spread(current)
-        outgoing, currents = pack(step, keeps, True, own, (None, currents), [])
+        outgoing, currents, current = first_pack(step, current, currents)
+        arrived_first = arrived_rest = exchange(outgoing)
         if lax.axis_size("lag") > 1:
-            outgoing, currents = pack(step, keeps, False, received, (outgoing, currents), after)
-        arrived = exchange(outgoing)
+            own, received, keeps = spread(current)
+            outgoing, currents = rest_pack(step, keeps, own, received, currents, after)
+            arrived_rest = exchange(outgoing)
         field = shifted(field)
         if step + 1 < steps:
             current = call(
@@ -299,7 +320,7 @@
                 [
                     (VMEM, high),
                     (HBM, low),
-                    (VMEM, arrived),
+                    (VMEM, arrived_first),
                     (VMEM, field),
                     (HBM, incident),
                     (HBM, self_inverse),
@@ -312,7 +333,7 @@
             field = call(
                 partial_kernel,
                 [(VMEM, column, f32)],
-                [(VMEM, high), (HBM, low), (VMEM, arrived), (VMEM, field), (VMEM, current)],
+                [(VMEM, high), (HBM, low), (VMEM, arrived_rest), (VMEM, field)],
                 [pltpu.VMEM(panel, bf16), DMA],
                 all_flops,
                 panel_bytes + arrived_bytes,
@@ -323,7 +344,7 @@
             field = call(
                 ahead_kernel,
                 [(HBM, column, f32)],
-                [(VMEM, high), (HBM, low), (VMEM, arrived), (VMEM, field)],
+                [(VMEM, high), (HBM, low), (VMEM, arrived_first), (VMEM, arrived_rest), (VMEM, field)],
                 [pltpu.VMEM(panel, bf16), pltpu.VMEM(column, f32), DMA((3,))],
                 all_flops,
                 panel_bytes + arrived_bytes,

time: 126 us -> 178 us (1.41)
  waiting for transfers between devices: 52.5 us -> 89.7 us
  starting transfers between devices: 30.6 us -> 55.9 us
  blocking collectives: 12.3 us -> 0 us
  local copies, waits for them, and re-layouts: 0.01 us -> 2.09 us
    all_to_all x4 -> x9, waiting for transfers between devices: 12.5 us -> 43.4 us  [exchange(): return lax.all_to_all(x, 'patch', split_axis=0, concat_axis=0, tiled=True)]
    all_to_all x4 -> x9, starting transfers between devices: 16.7 us -> 44.5 us  [exchange(): return lax.all_to_all(x, 'patch', split_axis=0, concat_axis=0, tiled=True)]
    all_to_all x1 -> x0, blocking collectives: 12.3 us -> none  [exchange(): return lax.all_to_all(x, 'patch', split_axis=0, concat_axis=0, tiled=True)]
    ppermute x4, waiting for transfers between devices: 5.13 us -> 13.8 us  [spread(): received = lax.ppermute(x, 'lag', pairs)]
    ppermute x4, starting transfers between devices: 8.72 us -> 6.3 us  [spread(): received = lax.ppermute(x, 'lag', pairs)]
    ppermute x4, waiting for transfers between devices: 34.9 us -> 32.6 us  [shifted(): return lax.ppermute(x, 'lag', [(i, i - 1) for i in range(1, sections)])]
    unnamed x2 -> x6, local copies, waits for them, and re-layouts: 0.01 us -> 2.09 us
  transfers between devices with their start and end apart: 12 -> 17, of which waited for: 11 -> 14; matrix products, arithmetic and copies ran while one was open for 0% -> 0% of each run, Pallas kernels for 8% -> 12%
where the time goes in v1:
time: 178 us; the launch traced here: 177 us
  waiting for transfers between devices  89.7 us (50%)
  starting transfers between devices  55.9 us (31%)
  Pallas kernels  27.8 us (16%)
  local copies, waits for them, and re-layouts  2.09 us (1%)
    all_to_all x9, starting transfers between devices, exchange(): return lax.all_to_all(x, 'patch', split_axis=0, concat_axis=0, tiled=True)  44.5 us
    all_to_all x9, waiting for transfers between devices, exchange(): return lax.all_to_all(x, 'patch', split_axis=0, concat_axis=0, tiled=True)  43.4 us
    ppermute x4, waiting for transfers between devices, shifted(): return lax.ppermute(x, 'lag', [(i, i - 1) for i in range(1, sections)])  32.6 us
    pallas_call x18, Pallas kernels, call(): run(*(pltpu.with_memory_space_constraint(x, space) for space, x in ins))  27.8 us
    ppermute x4, waiting for transfers between devices, spread(): received = lax.ppermute(x, 'lag', pairs)  13.8 us
    ppermute x4, starting transfers between devices, spread(): received = lax.ppermute(x, 'lag', pairs)  6.3 us
    ppermute x4, starting transfers between devices, shifted(): return lax.ppermute(x, 'lag', [(i, i - 1) for i in range(1, sections)])  5.17 us
  transfers between devices with their start and end apart: 17, of which 14 were waited for; matrix products, arithmetic and copies ran while one was open for 0% of the time, Pallas kernels for 12%

profile of v1, /device:TPU:0, one launch (start us, length us, event | category | flops | bytes accessed | tf_op | source)
XLA Modules:
  0.0 176.7 jit_solution(1070627806725694309)
XLA Ops:
  0.6 1.8 %shard_map.86.after = s32[16,1,128]{2,1,0:T(1,128)} custom-call(s32[1,1,56]{2,1,0:T(1,128)} %refs_1_.3, s32[64]{0:T(128)} %refs_2_.1), custom_call_target="tpu_custom_call" | custom-call | tf_op jit(solution)/shard_map/pallas_call | solution.py:26
  2.4 7.4 %all-to-all-start = ((s32[16,1,128]{2,1,0:T(1,128)}), s32[16,1,128]{2,1,0:T(1,128)S(1)}, u32[]{:S(2)}, u32[]{:S(2)}) async-start(s32[16,1,128]{2,1,0:T(1,128)} %shard_map.86.after), calls=%async_computation | async-start | bytes 16384 | tf_op jit(solution)/shard_map/all_to_all | solution.py:243
  9.8 1.5 shard_map.88.refs_1_
  11.3 4.8 %all-to-all-done.refs_0_ = s32[16,1,128]{2,1,0:T(1,128)S(1)} async-done(((s32[16,1,128]{2,1,0:T(1,128)}), s32[16,1,128]{2,1,0:T(1,128)S(1)}, u32[]{:S(2)}, u32[]{:S(2)}) %all-to-all-start) | async-done | bytes 8224 | tf_op jit(solution)/shard_map/all_to_all | solution.py:243
  17.3 3.6 %all-to-all-start.1 = ((bf16[16,128,128]{2,1,0:T(8,128)(2,1)}), bf16[16,128,128]{2,1,0:T(8,128)(2,1)S(1)}, u32[]{:S(2)}, u32[]{:S(2)}) async-start(bf16[16,128,128]{2,1,0:T(8,128)(2,1)} %get-tuple-element.26), calls=%async_computation.1 | async-start | bytes 1048576 | tf_op jit(solution)/shard_map/all_to_all | solution.py:243
  20.9 2.4 %collective-permute-start.1 = (bf16[512,128]{1,0:T(8,128)(2,1)S(1)}, bf16[512,128]{1,0:T(8,128)(2,1)S(1)}, u32[]{:S(2)}, u32[]{:S(2)}) collective-permute-start(bf16[512,128]{1,0:T(8,128)(2,1)S(1)} %get-tuple-element.27.refs_1_), channel_id=1, source_target_pairs={{0,16},{1,17},{2,18},{3,19},{4,20},{5,21},{6,22},{7,23},{8,24},{9,... | collective-permute-start | bytes 393224 | tf_op jit(solution)/shard_map/ppermute | solution.py:223
  23.3 3.2 %collective-permute-done.1.refs_2_ = bf16[512,128]{1,0:T(8,128)(2,1)S(1)} collective-permute-done((bf16[512,128]{1,0:T(8,128)(2,1)S(1)}, bf16[512,128]{1,0:T(8,128)(2,1)S(1)}, u32[]{:S(2)}, u32[]{:S(2)}) %collective-permute-start.1) | collective-permute-done | bytes 131104 | tf_op jit(solution)/shard_map/ppermute | solution.py:223
  26.7 8.7 %all-to-all-done.1.refs_2_ = bf16[16,128,128]{2,1,0:T(8,128)(2,1)S(1)} async-done(((bf16[16,128,128]{2,1,0:T(8,128)(2,1)}), bf16[16,128,128]{2,1,0:T(8,128)(2,1)S(1)}, u32[]{:S(2)}, u32[]{:S(2)}) %all-to-all-start.1) | async-done | bytes 524320 | tf_op jit(solution)/shard_map/all_to_all | solution.py:243
  35.3 4.0 %all-to-all-start.3 = ((bf16[16,128,128]{2,1,0:T(8,128)(2,1)}), bf16[16,128,128]{2,1,0:T(8,128)(2,1)S(1)}, u32[]{:S(2)}, u32[]{:S(2)}) async-start(bf16[16,128,128]{2,1,0:T(8,128)(2,1)} %get-tuple-element.31), calls=%async_computation.3 | async-start | bytes 1048576 | tf_op jit(solution)/shard_map/all_to_all | solution.py:243
  40.7 5.2 %shard_map.87 = (bf16[512,2048]{1,0:T(8,128)(2,1)S(1)}, bf16[512,2048]{1,0:T(8,128)(2,1)}) custom-call(s32[1,1,56]{2,1,0:T(1,128)} %refs_0_.3, s32[1,1,56]{2,1,0:T(1,128)} %refs_1_.3, s32[64]{0:T(128)} %refs_2_.1, f32[1,1,56,128,128]{4,3,2,1,0:T(8,128)} %refs_3_.1), custom_call_target="tpu_custom_call" | custom-call | bytes 7864320 | tf_op jit(solution)/shard_map/pallas_call | solution.py:26
  45.9 4.2 %collective-permute-done.refs_3_.field = f32[512,128]{1,0:T(8,128)S(1)} collective-permute-done((f32[512,128]{1,0:T(8,128)}, f32[512,128]{1,0:T(8,128)S(1)}, u32[]{:S(2)}, u32[]{:S(2)}) %collective-permute-start) | collective-permute-done | bytes 262176 | tf_op jit(solution)/shard_map/ppermute | solution.py:212
  50.1 3.4 %shard_map.90.refs_1_ = bf16[512,128]{1,0:T(8,128)(2,1)S(1)} custom-call(bf16[512,2048]{1,0:T(8,128)(2,1)S(1)} %get-tuple-element.24.refs_0_.high, bf16[512,2048]{1,0:T(8,128)(2,1)} %get-tuple-element.25.refs_1_.low_hbm, bf16[16,128,128]{2,1,0:T(8,128)(2,1)S(1)} %all-to-all-done.1.refs_2_, f32[512,128]{1,0:T(8,128)S(1)} %collective-permute-done.refs_3_.field, ...), custom_call_target="tpu_custom_call" | custom-call | flops 637534208 | bytes 4718592 | tf_op jit(solution)/shard_map/pallas_call | solution.py:26
  54.8 5.7 %all-to-all-start.2 = ((bf16[16,128,128]{2,1,0:T(8,128)(2,1)}), bf16[16,128,128]{2,1,0:T(8,128)(2,1)S(1)}, u32[]{:S(2)}, u32[]{:S(2)}) async-start(bf16[16,128,128]{2,1,0:T(8,128)(2,1)} %get-tuple-element.30), calls=%async_computation.2 | async-start | bytes 1048576 | tf_op jit(solution)/shard_map/all_to_all | solution.py:243
  60.5 1.3 collective-permute-start.3
  61.8 3.5 %collective-permute-done.3.refs_2_ = bf16[512,128]{1,0:T(8,128)(2,1)S(1)} collective-permute-done((bf16[512,128]{1,0:T(8,128)(2,1)S(1)}, bf16[512,128]{1,0:T(8,128)(2,1)S(1)}, u32[]{:S(2)}, u32[]{:S(2)}) %collective-permute-start.3) | collective-permute-done | bytes 131104 | tf_op jit(solution)/shard_map/ppermute | solution.py:223
  66.2 8.7 %all-to-all-done.2.refs_2_ = bf16[16,128,128]{2,1,0:T(8,128)(2,1)S(1)} async-done(((bf16[16,128,128]{2,1,0:T(8,128)(2,1)}), bf16[16,128,128]{2,1,0:T(8,128)(2,1)S(1)}, u32[]{:S(2)}, u32[]{:S(2)}) %all-to-all-start.2) | async-done | bytes 524320 | tf_op jit(solution)/shard_map/all_to_all | solution.py:243
  75.0 4.1 %all-to-all-start.5 = ((bf16[16,128,128]{2,1,0:T(8,128)(2,1)}), bf16[16,128,128]{2,1,0:T(8,128)(2,1)S(1)}, u32[]{:S(2)}, u32[]{:S(2)}) async-start(bf16[16,128,128]{2,1,0:T(8,128)(2,1)} %get-tuple-element.36), calls=%async_computation.5 | async-start | bytes 1048576 | tf_op jit(solution)/shard_map/all_to_all | solution.py:243
  80.4 9.4 %collective-permute-done.2.refs_3_.field = f32[512,128]{1,0:T(8,128)S(1)} collective-permute-done((f32[512,128]{1,0:T(8,128)}, f32[512,128]{1,0:T(8,128)S(1)}, u32[]{:S(2)}, u32[]{:S(2)}) %collective-permute-start.2) | collective-permute-done | bytes 262176 | tf_op jit(solution)/shard_map/ppermute | solution.py:212
  89.8 3.4 %shard_map.94.refs_1_ = bf16[512,128]{1,0:T(8,128)(2,1)S(1)} custom-call(bf16[512,2048]{1,0:T(8,128)(2,1)S(1)} %get-tuple-element.24.refs_0_.high, bf16[512,2048]{1,0:T(8,128)(2,1)} %get-tuple-element.25.refs_1_.low_hbm, bf16[16,128,128]{2,1,0:T(8,128)(2,1)S(1)} %all-to-all-done.2.refs_2_, f32[512,128]{1,0:T(8,128)S(1)} %collective-permute-done.2.refs_3_.field, ...), custom_call_target="tpu_custom_call" | custom-call | flops 637534208 | bytes 4718592 | tf_op jit(solution)/shard_map/pallas_call | solution.py:26
  94.5 5.7 %all-to-all-start.4 = ((bf16[16,128,128]{2,1,0:T(8,128)(2,1)}), bf16[16,128,128]{2,1,0:T(8,128)(2,1)S(1)}, u32[]{:S(2)}, u32[]{:S(2)}) async-start(bf16[16,128,128]{2,1,0:T(8,128)(2,1)} %get-tuple-element.35), calls=%async_computation.4 | async-start | bytes 1048576 | tf_op jit(solution)/shard_map/all_to_all | solution.py:243
  101.6 3.5 %collective-permute-done.5.refs_2_ = bf16[512,128]{1,0:T(8,128)(2,1)S(1)} collective-permute-done((bf16[512,128]{1,0:T(8,128)(2,1)S(1)}, bf16[512,128]{1,0:T(8,128)(2,1)S(1)}, u32[]{:S(2)}, u32[]{:S(2)}) %collective-permute-start.5) | collective-permute-done | bytes 131104 | tf_op jit(solution)/shard_map/ppermute | solution.py:223
  106.0 8.7 %all-to-all-done.4.refs_2_ = bf16[16,128,128]{2,1,0:T(8,128)(2,1)S(1)} async-done(((bf16[16,128,128]{2,1,0:T(8,128)(2,1)}), bf16[16,128,128]{2,1,0:T(8,128)(2,1)S(1)}, u32[]{:S(2)}, u32[]{:S(2)}) %all-to-all-start.4) | async-done | bytes 524320 | tf_op jit(solution)/shard_map/all_to_all | solution.py:243
  114.7 4.1 %all-to-all-start.6 = ((bf16[16,128,128]{2,1,0:T(8,128)(2,1)}), bf16[16,128,128]{2,1,0:T(8,128)(2,1)S(1)}, u32[]{:S(2)}, u32[]{:S(2)}) async-start(bf16[16,128,128]{2,1,0:T(8,128)(2,1)} %get-tuple-element.41), calls=%async_computation.6 | async-start | bytes 1048576 | tf_op jit(solution)/shard_map/all_to_all | solution.py:243
  120.1 9.4 %collective-permute-done.4.refs_3_.field = f32[512,128]{1,0:T(8,128)S(1)} collective-permute-done((f32[512,128]{1,0:T(8,128)}, f32[512,128]{1,0:T(8,128)S(1)}, u32[]{:S(2)}, u32[]{:S(2)}) %collective-permute-start.4) | collective-permute-done | bytes 262176 | tf_op jit(solution)/shard_map/ppermute | solution.py:212
  129.5 3.4 %shard_map.98.refs_1_ = bf16[512,128]{1,0:T(8,128)(2,1)S(1)} custom-call(bf16[512,2048]{1,0:T(8,128)(2,1)S(1)} %get-tuple-element.24.refs_0_.high, bf16[512,2048]{1,0:T(8,128)(2,1)} %get-tuple-element.25.refs_1_.low_hbm, bf16[16,128,128]{2,1,0:T(8,128)(2,1)S(1)} %all-to-all-done.4.refs_2_, f32[512,128]{1,0:T(8,128)S(1)} %collective-permute-done.4.refs_3_.field, ...), custom_call_target="tpu_custom_call" | custom-call | flops 637534208 | bytes 4718592 | tf_op jit(solution)/shard_map/pallas_call | solution.py:26
  134.2 5.7 %all-to-all-start.7 = ((bf16[16,128,128]{2,1,0:T(8,128)(2,1)}), bf16[16,128,128]{2,1,0:T(8,128)(2,1)S(1)}, u32[]{:S(2)}, u32[]{:S(2)}) async-start(bf16[16,128,128]{2,1,0:T(8,128)(2,1)} %get-tuple-element.44), calls=%async_computation.7 | async-start | bytes 1048576 | tf_op jit(solution)/shard_map/all_to_all | solution.py:243
  141.3 3.5 %collective-permute-done.6.refs_2_ = bf16[512,128]{1,0:T(8,128)(2,1)S(1)} collective-permute-done((bf16[512,128]{1,0:T(8,128)(2,1)S(1)}, bf16[512,128]{1,0:T(8,128)(2,1)S(1)}, u32[]{:S(2)}, u32[]{:S(2)}) %collective-permute-start.6) | collective-permute-done | bytes 131104 | tf_op jit(solution)/shard_map/ppermute | solution.py:223
  145.7 8.7 %all-to-all-done.7.arrived_first = bf16[16,128,128]{2,1,0:T(8,128)(2,1)S(1)} async-done(((bf16[16,128,128]{2,1,0:T(8,128)(2,1)}), bf16[16,128,128]{2,1,0:T(8,128)(2,1)S(1)}, u32[]{:S(2)}, u32[]{:S(2)}) %all-to-all-start.7) | async-done | bytes 524320 | tf_op jit(solution)/shard_map/all_to_all | solution.py:243
  154.4 4.1 %all-to-all-start.8 = ((bf16[16,128,128]{2,1,0:T(8,128)(2,1)}), bf16[16,128,128]{2,1,0:T(8,128)(2,1)S(1)}, u32[]{:S(2)}, u32[]{:S(2)}) async-start(bf16[16,128,128]{2,1,0:T(8,128)(2,1)} %get-tuple-element.45), calls=%async_computation.8 | async-start | bytes 1048576 | tf_op jit(solution)/shard_map/all_to_all | solution.py:243
  159.8 9.4 %collective-permute-done.7.field = f32[512,128]{1,0:T(8,128)S(1)} collective-permute-done((f32[512,128]{1,0:T(8,128)}, f32[512,128]{1,0:T(8,128)S(1)}, u32[]{:S(2)}, u32[]{:S(2)}) %collective-permute-start.7) | collective-permute-done | bytes 262176 | tf_op jit(solution)/shard_map/ppermute | solution.py:212
  169.2 3.7 %all-to-all-done.8.arrived_rest = bf16[16,128,128]{2,1,0:T(8,128)(2,1)S(1)} async-done(((bf16[16,128,128]{2,1,0:T(8,128)(2,1)}), bf16[16,128,128]{2,1,0:T(8,128)(2,1)S(1)}, u32[]{:S(2)}, u32[]{:S(2)}) %all-to-all-start.8) | async-done | bytes 524320 | tf_op jit(solution)/shard_map/all_to_all | solution.py:243
  173.0 3.5 %shard_map.103 = f32[512,128]{1,0:T(8,128)} custom-call(bf16[512,2048]{1,0:T(8,128)(2,1)S(1)} %get-tuple-element.24.refs_0_.high, bf16[512,2048]{1,0:T(8,128)(2,1)} %get-tuple-element.25.refs_1_.low_hbm, bf16[16,128,128]{2,1,0:T(8,128)(2,1)S(1)} %all-to-all-done.7.arrived_first, bf16[16,128,128]{2,1,0:T(8,128)(2,1)S(1)} %all-to-all-done.8.arrived_rest, ...), custom_call_target="tpu_custom_call" | custom-call | flops 536870912 | bytes 4718592 | tf_op jit(solution)/shard_map/pallas_call | solution.py:26
  (26 shorter events, 15.3 us)
Async XLA Ops:
  2.4 13.7 %all-to-all-start = ((s32[16,1,128]{2,1,0:T(1,128)}), s32[16,1,128]{2,1,0:T(1,128)S(1)}, u32[]{:S(2)}, u32[]{:S(2)}) async-start(s32[16,1,128]{2,1,0:T(1,128)} %shard_map.86.after), calls=%async_computation | async-start | bytes 16384 | tf_op jit(solution)/shard_map/all_to_all | solution.py:243
  17.3 18.0 %all-to-all-start.1 = ((bf16[16,128,128]{2,1,0:T(8,128)(2,1)}), bf16[16,128,128]{2,1,0:T(8,128)(2,1)S(1)}, u32[]{:S(2)}, u32[]{:S(2)}) async-start(bf16[16,128,128]{2,1,0:T(8,128)(2,1)} %get-tuple-element.26), calls=%async_computation.1 | async-start | bytes 1048576 | tf_op jit(solution)/shard_map/all_to_all | solution.py:243
  20.9 5.6 %collective-permute-start.1 = (bf16[512,128]{1,0:T(8,128)(2,1)S(1)}, bf16[512,128]{1,0:T(8,128)(2,1)S(1)}, u32[]{:S(2)}, u32[]{:S(2)}) collective-permute-start(bf16[512,128]{1,0:T(8,128)(2,1)S(1)} %get-tuple-element.27.refs_1_), channel_id=1, source_target_pairs={{0,16},{1,17},{2,18},{3,19},{4,20},{5,21},{6,22},{7,23},{8,24},{9,... | collective-permute-start | bytes 393224 | tf_op jit(solution)/shard_map/ppermute | solution.py:223
  35.3 19.4 %all-to-all-start.3 = ((bf16[16,128,128]{2,1,0:T(8,128)(2,1)}), bf16[16,128,128]{2,1,0:T(8,128)(2,1)S(1)}, u32[]{:S(2)}, u32[]{:S(2)}) async-start(bf16[16,128,128]{2,1,0:T(8,128)(2,1)} %get-tuple-element.31), calls=%async_computation.3 | async-start | bytes 1048576 | tf_op jit(solution)/shard_map/all_to_all | solution.py:243
  39.4 10.7 %collective-permute-start = (f32[512,128]{1,0:T(8,128)}, f32[512,128]{1,0:T(8,128)S(1)}, u32[]{:S(2)}, u32[]{:S(2)}) collective-permute-start(f32[512,128]{1,0:T(8,128)} %bitcast.field_hbm), channel_id=1, source_target_pairs={{16,0},{17,1},{18,2},{19,3},{20,4},{21,5},{22,6},{23,7},{24,8},{25... | collective-permute-start | bytes 786440 | tf_op jit(solution)/shard_map/ppermute | solution.py:212
  54.8 20.2 %all-to-all-start.2 = ((bf16[16,128,128]{2,1,0:T(8,128)(2,1)}), bf16[16,128,128]{2,1,0:T(8,128)(2,1)S(1)}, u32[]{:S(2)}, u32[]{:S(2)}) async-start(bf16[16,128,128]{2,1,0:T(8,128)(2,1)} %get-tuple-element.30), calls=%async_computation.2 | async-start | bytes 1048576 | tf_op jit(solution)/shard_map/all_to_all | solution.py:243
  60.5 4.9 %collective-permute-start.3 = (bf16[512,128]{1,0:T(8,128)(2,1)S(1)}, bf16[512,128]{1,0:T(8,128)(2,1)S(1)}, u32[]{:S(2)}, u32[]{:S(2)}) collective-permute-start(bf16[512,128]{1,0:T(8,128)(2,1)S(1)} %get-tuple-element.32.refs_1_), channel_id=1, source_target_pairs={{0,16},{1,17},{2,18},{3,19},{4,20},{5,21},{6,22},{7,23},{8,24},{9,... | collective-permute-start | bytes 393224 | tf_op jit(solution)/shard_map/ppermute | solution.py:223
  65.5 0.7 copy-start.1
  75.0 19.5 %all-to-all-start.5 = ((bf16[16,128,128]{2,1,0:T(8,128)(2,1)}), bf16[16,128,128]{2,1,0:T(8,128)(2,1)S(1)}, u32[]{:S(2)}, u32[]{:S(2)}) async-start(bf16[16,128,128]{2,1,0:T(8,128)(2,1)} %get-tuple-element.36), calls=%async_computation.5 | async-start | bytes 1048576 | tf_op jit(solution)/shard_map/all_to_all | solution.py:243
  79.1 10.7 %collective-permute-start.2 = (f32[512,128]{1,0:T(8,128)}, f32[512,128]{1,0:T(8,128)S(1)}, u32[]{:S(2)}, u32[]{:S(2)}) collective-permute-start(f32[512,128]{1,0:T(8,128)} %copy-done.1), channel_id=1, source_target_pairs={{16,0},{17,1},{18,2},{19,3},{20,4},{21,5},{22,6},{23,7},{24,8},{25... | collective-permute-start | bytes 786440 | tf_op jit(solution)/shard_map/ppermute | solution.py:212
  94.5 20.2 %all-to-all-start.4 = ((bf16[16,128,128]{2,1,0:T(8,128)(2,1)}), bf16[16,128,128]{2,1,0:T(8,128)(2,1)S(1)}, u32[]{:S(2)}, u32[]{:S(2)}) async-start(bf16[16,128,128]{2,1,0:T(8,128)(2,1)} %get-tuple-element.35), calls=%async_computation.4 | async-start | bytes 1048576 | tf_op jit(solution)/shard_map/all_to_all | solution.py:243
  100.2 4.9 %collective-permute-start.5 = (bf16[512,128]{1,0:T(8,128)(2,1)S(1)}, bf16[512,128]{1,0:T(8,128)(2,1)S(1)}, u32[]{:S(2)}, u32[]{:S(2)}) collective-permute-start(bf16[512,128]{1,0:T(8,128)(2,1)S(1)} %get-tuple-element.37.refs_1_), channel_id=1, source_target_pairs={{0,16},{1,17},{2,18},{3,19},{4,20},{5,21},{6,22},{7,23},{8,24},{9,... | collective-permute-start | bytes 393224 | tf_op jit(solution)/shard_map/ppermute | solution.py:223
  105.3 0.7 copy-start.2
  114.7 19.5 %all-to-all-start.6 = ((bf16[16,128,128]{2,1,0:T(8,128)(2,1)}), bf16[16,128,128]{2,1,0:T(8,128)(2,1)S(1)}, u32[]{:S(2)}, u32[]{:S(2)}) async-start(bf16[16,128,128]{2,1,0:T(8,128)(2,1)} %get-tuple-element.41), calls=%async_computation.6 | async-start | bytes 1048576 | tf_op jit(solution)/shard_map/all_to_all | solution.py:243
  118.8 10.7 %collective-permute-start.4 = (f32[512,128]{1,0:T(8,128)}, f32[512,128]{1,0:T(8,128)S(1)}, u32[]{:S(2)}, u32[]{:S(2)}) collective-permute-start(f32[512,128]{1,0:T(8,128)} %copy-done.2), channel_id=1, source_target_pairs={{16,0},{17,1},{18,2},{19,3},{20,4},{21,5},{22,6},{23,7},{24,8},{25... | collective-permute-start | bytes 786440 | tf_op jit(solution)/shard_map/ppermute | solution.py:212
  134.2 20.2 %all-to-all-start.7 = ((bf16[16,128,128]{2,1,0:T(8,128)(2,1)}), bf16[16,128,128]{2,1,0:T(8,128)(2,1)S(1)}, u32[]{:S(2)}, u32[]{:S(2)}) async-start(bf16[16,128,128]{2,1,0:T(8,128)(2,1)} %get-tuple-element.44), calls=%async_computation.7 | async-start | bytes 1048576 | tf_op jit(solution)/shard_map/all_to_all | solution.py:243
  139.9 4.9 %collective-permute-start.6 = (bf16[512,128]{1,0:T(8,128)(2,1)S(1)}, bf16[512,128]{1,0:T(8,128)(2,1)S(1)}, u32[]{:S(2)}, u32[]{:S(2)}) collective-permute-start(bf16[512,128]{1,0:T(8,128)(2,1)S(1)} %get-tuple-element.40.refs_1_), channel_id=1, source_target_pairs={{0,16},{1,17},{2,18},{3,19},{4,20},{5,21},{6,22},{7,23},{8,24},{9,... | collective-permute-start | bytes 393224 | tf_op jit(solution)/shard_map/ppermute | solution.py:223
  145.0 0.7 copy-start
  154.4 18.6 %all-to-all-start.8 = ((bf16[16,128,128]{2,1,0:T(8,128)(2,1)}), bf16[16,128,128]{2,1,0:T(8,128)(2,1)S(1)}, u32[]{:S(2)}, u32[]{:S(2)}) async-start(bf16[16,128,128]{2,1,0:T(8,128)(2,1)} %get-tuple-element.45), calls=%async_computation.8 | async-start | bytes 1048576 | tf_op jit(solution)/shard_map/all_to_all | solution.py:243
  158.5 10.7 %collective-permute-start.7 = (f32[512,128]{1,0:T(8,128)}, f32[512,128]{1,0:T(8,128)S(1)}, u32[]{:S(2)}, u32[]{:S(2)}) collective-permute-start(f32[512,128]{1,0:T(8,128)} %copy-done), channel_id=1, source_target_pairs={{16,0},{17,1},{18,2},{19,3},{20,4},{21,5},{22,6},{23,7},{24,8},{25... | collective-permute-start | bytes 786440 | tf_op jit(solution)/shard_map/ppermute | solution.py:212

commit v2 on v0

--- a/solution.py
+++ b/solution.py
@@ -34,13 +34,16 @@
     return copies
 
 
-def request_kernel(per_patch, sources_hbm, owner_hbm, wanted_hbm, wanted, sources, owner_map, sems):
+def request_kernel(
+    per_patch, sources_hbm, owner_hbm, field_hbm, wanted_hbm, field, wanted, sources, owner_map, sems
+):
     copies = started(
         (sources_hbm, sources, sems.at[0]),
         (owner_hbm, owner_map, sems.at[1]),
+        (field_hbm, field, sems.at[2]),
     )
     patch = lax.broadcasted_iota(jnp.int32, wanted.shape, 0)
-    for copy in copies:
+    for copy in copies[:2]:
         copy.wait()
 
     def entry(j, table):
@@ -53,6 +56,7 @@
         0, sources.shape[2], entry, jnp.full(wanted.shape, -1, jnp.int32), unroll=8
     )
     started((wanted, wanted_hbm, sems.at[0]))[0].wait()
+    copies[2].wait()
 
 
 def panel_kernel(
@@ -116,32 +120,24 @@
     return jnp.concatenate(parts, axis=0).astype(jnp.bfloat16)
 
 
-def products(high, low_hbm, arrived, low, sem, parts=1):
+def product(high, low_hbm, arrived, low, sem):
     patches, size, columns = arrived.shape
     (copy,) = started((low_hbm, low, sem))
-    rows = high.shape[0] // parts
-    for part in range(parts):
-        here = slice(part * rows, (part + 1) * rows)
-        flat = arrived[...].reshape(patches * size, columns)
-        fresh = jnp.dot(high[here], flat, preferred_element_type=jnp.float32)
-        if part == 0:
-            copy.wait()
-        yield here, fresh + jnp.dot(low[here], flat, preferred_element_type=jnp.float32)
-
-
-def first_kernel(incident_hbm, field_hbm, inverse_hbm, after, current, incident, field, inverse, sems):
-    del after
-
-    @pl.when(lax.axis_index("lag") == 0)
-    def _():
-        copies = started(
-            (incident_hbm.at[0], incident, sems.at[0]),
-            (inverse_hbm, inverse, sems.at[1]),
-            (field_hbm, field, sems.at[2]),
-        )
-        for copy in copies:
-            copy.wait()
-        current[...] = solved(incident[...].astype(jnp.float32) - field[...], inverse)
+    flat = arrived[...].reshape(patches * size, columns)
+    fresh = jnp.dot(high[...], flat, preferred_element_type=jnp.float32)
+    copy.wait()
+    return fresh + jnp.dot(low[...], flat, preferred_element_type=jnp.float32)
+
+
+def first_kernel(keeps, incident_hbm, own, received, inverse_hbm, current, incident, inverse, sems):
+    copies = started(
+        (incident_hbm.at[0], incident, sems.at[0]),
+        (inverse_hbm, inverse, sems.at[1]),
+    )
+    field = jnp.where(lax.axis_index("lag") < keeps, own[...], received[...])
+    for copy in copies:
+        copy.wait()
+    current[...] = solved(incident[...].astype(jnp.float32) - field, inverse)
 
 
 def solve_kernel(
@@ -153,7 +149,7 @@
             (incident_hbm.at[step], incident, sems.at[0]),
             (inverse_hbm, inverse, sems.at[1]),
         )
-        ((_, fresh),) = products(high, low_hbm, arrived, low, sems.at[2])
+        fresh = product(high, low_hbm, arrived, low, sems.at[2])
         for copy in copies:
             copy.wait()
         excess = incident[...].astype(jnp.float32) - (field[...] + fresh)
@@ -165,15 +161,20 @@
 
     @pl.when(lax.axis_index("lag") > 0)
     def _():
-        ((_, fresh),) = products(high, low_hbm, arrived, low, sem)
+        fresh = product(high, low_hbm, arrived, low, sem)
         partial[...] = field[...] + fresh
 
 
-def ahead_kernel(high, low_hbm, arrived, field, ahead_hbm, low, ahead, sems):
+def ahead_kernel(high, arrived, field, ahead_hbm, ahead, sems):
+    patches, size, columns = arrived.shape
+    rows = ahead.shape[0] // sems.shape[0]
     copies = []
-    for here, fresh in products(high, low_hbm, arrived, low, sems.at[0], 2):
-        ahead[here] = field[here] + fresh
-        copies += started((ahead.at[here], ahead_hbm.at[here], sems.at[len(copies) + 1]))
+    for part in range(sems.shape[0]):
+        here = pl.ds(part * rows, rows)
+        flat = arrived[...].reshape(patches * size, columns)
+        fresh = jnp.dot(high[here, :], flat, preferred_element_type=jnp.float32)
+        ahead[here, :] = field[here, :] + fresh
+        copies += started((ahead.at[here], ahead_hbm.at[here], sems.at[part]))
     for copy in copies:
         copy.wait()
 
@@ -223,14 +224,12 @@
     solve_flops = 12 * unknowns * size * columns
     panel_bytes = 4 * unknowns * patches * size
     column = (unknowns, columns)
-
-    column_bytes = 4 * unknowns * columns
     arrived_bytes = 2 * patches * size * columns
 
     def exchange(x):
         return lax.all_to_all(x, "patch", split_axis=0, concat_axis=0, tiled=True)
 
-    def pack(step, keeps, early, current, filled, after):
+    def pack(step, keeps, early, current, filled, after=()):
         held = [x for x in filled if x is not None]
         aliases = {}
         for out, x in enumerate(filled):
@@ -244,24 +243,25 @@
             aliases=aliases,
         )
 
-    wanted = call(
+    wanted, first_field = call(
         lambda *refs: request_kernel(per_patch, *refs),
-        [(HBM, (patches, 1, 128), jnp.int32)],
-        [(HBM, block_sources), (HBM, owner_map)],
+        [(HBM, (patches, 1, 128), jnp.int32), (VMEM, column, f32)],
+        [(HBM, block_sources), (HBM, owner_map), (HBM, pending[0])],
         [
             pltpu.VMEM((patches, 1, 128), jnp.int32),
             pltpu.SMEM(block_sources.shape, jnp.int32),
             pltpu.SMEM(owner_map.shape, jnp.int32),
-            DMA((2,)),
+            DMA((3,)),
         ],
     )
     asked = exchange(wanted)
+    own, received, keeps = spread(first_field)
     solve_scratch = [pltpu.VMEM(column, bf16), pltpu.VMEM(self_inverse.shape, f32), DMA((3,))]
     current = call(
-        first_kernel,
+        lambda *refs: first_kernel(keeps, *refs),
         [(VMEM, column, bf16)],
-        [(HBM, incident), (HBM, pending[0]), (HBM, self_inverse), (HBM, wanted)],
-        [solve_scratch[0], pltpu.VMEM(column, f32), *solve_scratch[1:]],
+        [(HBM, incident), (VMEM, own), (VMEM, received), (HBM, self_inverse)],
+        solve_scratch,
         solve_flops,
     )
     chunk = max(n for n in range(1, 9) if listed % n == 0)
@@ -283,13 +283,13 @@
     )
 
     field = pending[0]
-    currents = None
-    after = []
+    outgoing, currents = pack(0, lax.axis_size("lag"), True, current, (None, None))
     for step in range(steps):
-        own, received, keeps = spread(current)
-        outgoing, currents = pack(step, keeps, True, own, (None, currents), [])
-        if lax.axis_size("lag") > 1:
-            outgoing, currents = pack(step, keeps, False, received, (outgoing, currents), after)
+        if step > 0:
+            own, received, keeps = spread(current)
+            outgoing, currents = pack(step, keeps, True, own, (None, currents))
+            if lax.axis_size("lag") > 1:
+                outgoing, currents = pack(step, keeps, False, received, (outgoing, currents), [field])
         arrived = exchange(outgoing)
         field = shifted(field)
         if step + 1 < steps:
@@ -318,13 +318,12 @@
                 panel_bytes + arrived_bytes,
                 panel_bytes + arrived_bytes,
             )
-            after = [field]
         else:
             field = call(
                 ahead_kernel,
                 [(HBM, column, f32)],
-                [(VMEM, high), (HBM, low), (VMEM, arrived), (VMEM, field)],
-                [pltpu.VMEM(panel, bf16), pltpu.VMEM(column, f32), DMA((3,))],
+                [(VMEM, high), (VMEM, arrived), (VMEM, field)],
+                [pltpu.VMEM(column, f32), DMA((2,))],
                 all_flops,
                 panel_bytes + arrived_bytes,
                 panel_bytes + arrived_bytes,

time: 126 us -> 124 us (0.984)
  blocking collectives: 12.3 us -> 0 us
  starting transfers between devices: 30.6 us -> 38 us
  waiting for transfers between devices: 52.5 us -> 57.4 us
  Pallas kernels: 28.2 us -> 25.7 us
    all_to_all x1 -> x0, blocking collectives: 12.3 us -> none  [exchange(): return lax.all_to_all(x, 'patch', split_axis=0, concat_axis=0, tiled=True)]
    all_to_all x4 -> x5, starting transfers between devices: 16.7 us -> 22.6 us  [exchange(): return lax.all_to_all(x, 'patch', split_axis=0, concat_axis=0, tiled=True)]
    all_to_all x4 -> x5, waiting for transfers between devices: 12.5 us -> 17.3 us  [exchange(): return lax.all_to_all(x, 'patch', split_axis=0, concat_axis=0, tiled=True)]
    pallas_call x18 -> x17, Pallas kernels: 28.2 us -> 25.7 us  [call(): run(*(pltpu.with_memory_space_constraint(x, space) for space, x in ins))]
    ppermute x4, starting transfers between devices: 8.72 us -> 10.2 us  [spread(): received = lax.ppermute(x, 'lag', pairs)]
  transfers between devices with their start and end apart: 12 -> 13, of which waited for: 11 -> 12; matrix products, arithmetic and copies ran while one was open for 0% -> 0% of each run, Pallas kernels for 8% -> 9%
where the time goes in v2:
time: 124 us; the launch traced here: 122 us
  waiting for transfers between devices  57.4 us (46%)
  starting transfers between devices  38 us (31%)
  Pallas kernels  25.7 us (21%)
    ppermute x4, waiting for transfers between devices, shifted(): return lax.ppermute(x, 'lag', [(i, i - 1) for i in range(1, sections)])  34.9 us
    pallas_call x17, Pallas kernels, call(): run(*(pltpu.with_memory_space_constraint(x, space) for space, x in ins))  25.7 us
    all_to_all x5, starting transfers between devices, exchange(): return lax.all_to_all(x, 'patch', split_axis=0, concat_axis=0, tiled=True)  22.6 us
    all_to_all x5, waiting for transfers between devices, exchange(): return lax.all_to_all(x, 'patch', split_axis=0, concat_axis=0, tiled=True)  17.3 us
    ppermute x4, starting transfers between devices, spread(): received = lax.ppermute(x, 'lag', pairs)  10.2 us
    ppermute x4, starting transfers between devices, shifted(): return lax.ppermute(x, 'lag', [(i, i - 1) for i in range(1, sections)])  5.17 us
    ppermute x4, waiting for transfers between devices, spread(): received = lax.ppermute(x, 'lag', pairs)  5.13 us
  transfers between devices with their start and end apart: 13, of which 12 were waited for; matrix products, arithmetic and copies ran while one was open for 0% of the time, Pallas kernels for 9%

profile of v2, /device:TPU:0, one launch (start us, length us, event | category | flops | bytes accessed | tf_op | source)
XLA Modules:
  0.0 122.2 jit_solution(17503975714069680952)
XLA Ops:
  0.6 1.9 %shard_map.86 = (s32[16,1,128]{2,1,0:T(1,128)}, f32[512,128]{1,0:T(8,128)S(1)}) custom-call(s32[1,1,56]{2,1,0:T(1,128)} %refs_1_.3, s32[64]{0:T(128)} %refs_2_.1, f32[512,128]{1,0:T(8,128)} %bitcast.3), custom_call_target="tpu_custom_call" | custom-call | tf_op jit(solution)/shard_map/pallas_call | solution.py:26
  2.6 4.9 %collective-permute-start = (f32[512,128]{1,0:T(8,128)S(1)}, f32[512,128]{1,0:T(8,128)S(1)}, u32[]{:S(2)}, u32[]{:S(2)}) collective-permute-start(f32[512,128]{1,0:T(8,128)S(1)} %get-tuple-element.23.refs_1_), channel_id=1, source_target_pairs={{0,16},{1,17},{2,18},{3,19},{4,20},{5,21},{6,22},{7,23},{8,24},{9,... | collective-permute-start | bytes 786440 | tf_op jit(solution)/shard_map/ppermute | solution.py:212
  7.5 5.9 %all-to-all-start = ((s32[16,1,128]{2,1,0:T(1,128)}), s32[16,1,128]{2,1,0:T(1,128)S(1)}, u32[]{:S(2)}, u32[]{:S(2)}) async-start(s32[16,1,128]{2,1,0:T(1,128)} %get-tuple-element.20), calls=%async_computation | async-start | bytes 16384 | tf_op jit(solution)/shard_map/all_to_all | solution.py:230
  13.4 1.4 %shard_map.88.refs_1_ = bf16[512,128]{1,0:T(8,128)(2,1)S(1)} custom-call(bf16[4,512,128]{2,1,0:T(8,128)(2,1)} %refs_4_.5, f32[512,128]{1,0:T(8,128)S(1)} %get-tuple-element.23.refs_1_, f32[512,128]{1,0:T(8,128)S(1)} %collective-permute-done.refs_2_, f32[4,128,128]{2,1,0:T(8,128)} %refs_5_.5), custom_call_target="tpu_custom_call" | custom-call | flops 100663296 | tf_op jit(solution)/shard_map/pallas_call | solution.py:26
  14.9 4.9 %all-to-all-done.refs_0_ = s32[16,1,128]{2,1,0:T(1,128)S(1)} async-done(((s32[16,1,128]{2,1,0:T(1,128)}), s32[16,1,128]{2,1,0:T(1,128)S(1)}, u32[]{:S(2)}, u32[]{:S(2)}) %all-to-all-start) | async-done | bytes 8224 | tf_op jit(solution)/shard_map/all_to_all | solution.py:230
  20.9 3.6 %all-to-all-start.1 = ((bf16[16,128,128]{2,1,0:T(8,128)(2,1)}), bf16[16,128,128]{2,1,0:T(8,128)(2,1)S(1)}, u32[]{:S(2)}, u32[]{:S(2)}) async-start(bf16[16,128,128]{2,1,0:T(8,128)(2,1)} %get-tuple-element.24), calls=%async_computation.1 | async-start | bytes 1048576 | tf_op jit(solution)/shard_map/all_to_all | solution.py:230
  24.5 1.3 %collective-permute-start.1 = (f32[512,128]{1,0:T(8,128)S(1)}, f32[512,128]{1,0:T(8,128)S(1)}, u32[]{:S(2)}, u32[]{:S(2)}) collective-permute-start(f32[512,128]{1,0:T(8,128)S(1)} %bitcast.4), channel_id=1, source_target_pairs={{16,0},{17,1},{18,2},{19,3},{20,4},{21,5},{22,6},{23,7},{24,8},{25... | collective-permute-start | bytes 786440 | tf_op jit(solution)/shard_map/ppermute | solution.py:201
  25.8 5.2 %shard_map.87 = (bf16[512,2048]{1,0:T(8,128)(2,1)S(1)}, bf16[512,2048]{1,0:T(8,128)(2,1)}) custom-call(s32[1,1,56]{2,1,0:T(1,128)} %refs_0_.4, s32[1,1,56]{2,1,0:T(1,128)} %refs_1_.3, s32[64]{0:T(128)} %refs_2_.1, f32[1,1,56,128,128]{4,3,2,1,0:T(8,128)} %refs_3_.2), custom_call_target="tpu_custom_call" | custom-call | bytes 7864320 | tf_op jit(solution)/shard_map/pallas_call | solution.py:26
  31.1 3.9 %collective-permute-done.1.refs_3_.field = f32[512,128]{1,0:T(8,128)S(1)} collective-permute-done((f32[512,128]{1,0:T(8,128)S(1)}, f32[512,128]{1,0:T(8,128)S(1)}, u32[]{:S(2)}, u32[]{:S(2)}) %collective-permute-start.1) | collective-permute-done | bytes 262176 | tf_op jit(solution)/shard_map/ppermute | solution.py:201
  34.9 4.0 %all-to-all-done.1.refs_2_.arrived = bf16[16,128,128]{2,1,0:T(8,128)(2,1)S(1)} async-done(((bf16[16,128,128]{2,1,0:T(8,128)(2,1)}), bf16[16,128,128]{2,1,0:T(8,128)(2,1)S(1)}, u32[]{:S(2)}, u32[]{:S(2)}) %all-to-all-start.1) | async-done | bytes 524320 | tf_op jit(solution)/shard_map/all_to_all | solution.py:230
  38.9 3.4 %shard_map.90.after.refs_1_ = bf16[512,128]{1,0:T(8,128)(2,1)S(1)} custom-call(bf16[512,2048]{1,0:T(8,128)(2,1)S(1)} %get-tuple-element.21.refs_0_.high, bf16[512,2048]{1,0:T(8,128)(2,1)} %get-tuple-element.22.refs_1_.low_hbm, bf16[16,128,128]{2,1,0:T(8,128)(2,1)S(1)} %all-to-all-done.1.refs_2_.arrived, f32[512,128]{1,0:T(8,128)S(1)} %collective-permute-done.1.refs_3_.field, ...), custom_call_target="tpu_custom_call" | custom-call | flops 637534208 | bytes 4718592 | tf_op jit(solution)/shard_map/pallas_call | solution.py:26
  42.4 1.3 %collective-permute-start.2 = (bf16[512,128]{1,0:T(8,128)(2,1)S(1)}, bf16[512,128]{1,0:T(8,128)(2,1)S(1)}, u32[]{:S(2)}, u32[]{:S(2)}) collective-permute-start(bf16[512,128]{1,0:T(8,128)(2,1)S(1)} %shard_map.90.after.refs_1_), channel_id=1, source_target_pairs={{0,16},{1,17},{2,18},{3,19},{4,20},{5,21},{6,22},{7,23},{8,24},{9,... | collective-permute-start | bytes 393224 | tf_op jit(solution)/shard_map/ppermute | solution.py:212
  44.9 2.0 %collective-permute-done.2.refs_1_ = bf16[512,128]{1,0:T(8,128)(2,1)S(1)} collective-permute-done((bf16[512,128]{1,0:T(8,128)(2,1)S(1)}, bf16[512,128]{1,0:T(8,128)(2,1)S(1)}, u32[]{:S(2)}, u32[]{:S(2)}) %collective-permute-start.2) | collective-permute-done | bytes 131104 | tf_op jit(solution)/shard_map/ppermute | solution.py:212
  47.0 4.3 %all-to-all-start.2 = ((bf16[16,128,128]{2,1,0:T(8,128)(2,1)}), bf16[16,128,128]{2,1,0:T(8,128)(2,1)S(1)}, u32[]{:S(2)}, u32[]{:S(2)}) async-start(bf16[16,128,128]{2,1,0:T(8,128)(2,1)} %get-tuple-element.28), calls=%async_computation.2 | async-start | bytes 1048576 | tf_op jit(solution)/shard_map/all_to_all | solution.py:230
  51.4 1.3 %collective-permute-start.3 = (f32[512,128]{1,0:T(8,128)S(1)}, f32[512,128]{1,0:T(8,128)S(1)}, u32[]{:S(2)}, u32[]{:S(2)}) collective-permute-start(f32[512,128]{1,0:T(8,128)S(1)} %shard_map.91.refs_2_), channel_id=1, source_target_pairs={{16,0},{17,1},{18,2},{19,3},{20,4},{21,5},{22,6},{23,7},{24,8},{25... | collective-permute-start | bytes 786440 | tf_op jit(solution)/shard_map/ppermute | solution.py:201
  52.7 10.3 %collective-permute-done.3.refs_3_.field = f32[512,128]{1,0:T(8,128)S(1)} collective-permute-done((f32[512,128]{1,0:T(8,128)S(1)}, f32[512,128]{1,0:T(8,128)S(1)}, u32[]{:S(2)}, u32[]{:S(2)}) %collective-permute-start.3) | collective-permute-done | bytes 262176 | tf_op jit(solution)/shard_map/ppermute | solution.py:201
  63.0 2.8 %all-to-all-done.2.refs_2_.arrived = bf16[16,128,128]{2,1,0:T(8,128)(2,1)S(1)} async-done(((bf16[16,128,128]{2,1,0:T(8,128)(2,1)}), bf16[16,128,128]{2,1,0:T(8,128)(2,1)S(1)}, u32[]{:S(2)}, u32[]{:S(2)}) %all-to-all-start.2) | async-done | bytes 524320 | tf_op jit(solution)/shard_map/all_to_all | solution.py:230
  65.8 3.4 %shard_map.94.after.refs_1_ = bf16[512,128]{1,0:T(8,128)(2,1)S(1)} custom-call(bf16[512,2048]{1,0:T(8,128)(2,1)S(1)} %get-tuple-element.21.refs_0_.high, bf16[512,2048]{1,0:T(8,128)(2,1)} %get-tuple-element.22.refs_1_.low_hbm, bf16[16,128,128]{2,1,0:T(8,128)(2,1)S(1)} %all-to-all-done.2.refs_2_.arrived, f32[512,128]{1,0:T(8,128)S(1)} %collective-permute-done.3.refs_3_.field, ...), custom_call_target="tpu_custom_call" | custom-call | flops 637534208 | bytes 4718592 | tf_op jit(solution)/shard_map/pallas_call | solution.py:26
  69.3 2.0 %collective-permute-start.4 = (bf16[512,128]{1,0:T(8,128)(2,1)S(1)}, bf16[512,128]{1,0:T(8,128)(2,1)S(1)}, u32[]{:S(2)}, u32[]{:S(2)}) collective-permute-start(bf16[512,128]{1,0:T(8,128)(2,1)S(1)} %shard_map.94.after.refs_1_), channel_id=1, source_target_pairs={{0,16},{1,17},{2,18},{3,19},{4,20},{5,21},{6,22},{7,23},{8,24},{9,... | collective-permute-start | bytes 393224 | tf_op jit(solution)/shard_map/ppermute | solution.py:212
  72.5 1.7 %collective-permute-done.4.refs_1_ = bf16[512,128]{1,0:T(8,128)(2,1)S(1)} collective-permute-done((bf16[512,128]{1,0:T(8,128)(2,1)S(1)}, bf16[512,128]{1,0:T(8,128)(2,1)S(1)}, u32[]{:S(2)}, u32[]{:S(2)}) %collective-permute-start.4) | collective-permute-done | bytes 131104 | tf_op jit(solution)/shard_map/ppermute | solution.py:212
  74.4 4.4 %all-to-all-start.3 = ((bf16[16,128,128]{2,1,0:T(8,128)(2,1)}), bf16[16,128,128]{2,1,0:T(8,128)(2,1)S(1)}, u32[]{:S(2)}, u32[]{:S(2)}) async-start(bf16[16,128,128]{2,1,0:T(8,128)(2,1)} %get-tuple-element.32), calls=%async_computation.3 | async-start | bytes 1048576 | tf_op jit(solution)/shard_map/all_to_all | solution.py:230
  78.8 1.3 %collective-permute-start.5 = (f32[512,128]{1,0:T(8,128)S(1)}, f32[512,128]{1,0:T(8,128)S(1)}, u32[]{:S(2)}, u32[]{:S(2)}) collective-permute-start(f32[512,128]{1,0:T(8,128)S(1)} %shard_map.95.refs_2_), channel_id=1, source_target_pairs={{16,0},{17,1},{18,2},{19,3},{20,4},{21,5},{22,6},{23,7},{24,8},{25... | collective-permute-start | bytes 786440 | tf_op jit(solution)/shard_map/ppermute | solution.py:201
  80.1 10.3 %collective-permute-done.5.refs_3_.field = f32[512,128]{1,0:T(8,128)S(1)} collective-permute-done((f32[512,128]{1,0:T(8,128)S(1)}, f32[512,128]{1,0:T(8,128)S(1)}, u32[]{:S(2)}, u32[]{:S(2)}) %collective-permute-start.5) | collective-permute-done | bytes 262176 | tf_op jit(solution)/shard_map/ppermute | solution.py:201
  90.4 2.8 %all-to-all-done.3.refs_2_.arrived = bf16[16,128,128]{2,1,0:T(8,128)(2,1)S(1)} async-done(((bf16[16,128,128]{2,1,0:T(8,128)(2,1)}), bf16[16,128,128]{2,1,0:T(8,128)(2,1)S(1)}, u32[]{:S(2)}, u32[]{:S(2)}) %all-to-all-start.3) | async-done | bytes 524320 | tf_op jit(solution)/shard_map/all_to_all | solution.py:230
  93.2 3.4 %shard_map.98.after.refs_1_ = bf16[512,128]{1,0:T(8,128)(2,1)S(1)} custom-call(bf16[512,2048]{1,0:T(8,128)(2,1)S(1)} %get-tuple-element.21.refs_0_.high, bf16[512,2048]{1,0:T(8,128)(2,1)} %get-tuple-element.22.refs_1_.low_hbm, bf16[16,128,128]{2,1,0:T(8,128)(2,1)S(1)} %all-to-all-done.3.refs_2_.arrived, f32[512,128]{1,0:T(8,128)S(1)} %collective-permute-done.5.refs_3_.field, ...), custom_call_target="tpu_custom_call" | custom-call | flops 637534208 | bytes 4718592 | tf_op jit(solution)/shard_map/pallas_call | solution.py:26
  96.7 2.0 %collective-permute-start.6 = (bf16[512,128]{1,0:T(8,128)(2,1)S(1)}, bf16[512,128]{1,0:T(8,128)(2,1)S(1)}, u32[]{:S(2)}, u32[]{:S(2)}) collective-permute-start(bf16[512,128]{1,0:T(8,128)(2,1)S(1)} %shard_map.98.after.refs_1_), channel_id=1, source_target_pairs={{0,16},{1,17},{2,18},{3,19},{4,20},{5,21},{6,22},{7,23},{8,24},{9,... | collective-permute-start | bytes 393224 | tf_op jit(solution)/shard_map/ppermute | solution.py:212
  100.1 1.5 %collective-permute-done.6.refs_1_ = bf16[512,128]{1,0:T(8,128)(2,1)S(1)} collective-permute-done((bf16[512,128]{1,0:T(8,128)(2,1)S(1)}, bf16[512,128]{1,0:T(8,128)(2,1)S(1)}, u32[]{:S(2)}, u32[]{:S(2)}) %collective-permute-start.6) | collective-permute-done | bytes 131104 | tf_op jit(solution)/shard_map/ppermute | solution.py:212
  101.8 4.4 %all-to-all-start.4 = ((bf16[16,128,128]{2,1,0:T(8,128)(2,1)}), bf16[16,128,128]{2,1,0:T(8,128)(2,1)S(1)}, u32[]{:S(2)}, u32[]{:S(2)}) async-start(bf16[16,128,128]{2,1,0:T(8,128)(2,1)} %get-tuple-element.37), calls=%async_computation.4 | async-start | bytes 1048576 | tf_op jit(solution)/shard_map/all_to_all | solution.py:230
  106.2 1.3 %collective-permute-start.7 = (f32[512,128]{1,0:T(8,128)S(1)}, f32[512,128]{1,0:T(8,128)S(1)}, u32[]{:S(2)}, u32[]{:S(2)}) collective-permute-start(f32[512,128]{1,0:T(8,128)S(1)} %shard_map.99.refs_2_), channel_id=1, source_target_pairs={{16,0},{17,1},{18,2},{19,3},{20,4},{21,5},{22,6},{23,7},{24,8},{25... | collective-permute-start | bytes 786440 | tf_op jit(solution)/shard_map/ppermute | solution.py:201
  107.5 10.3 %collective-permute-done.7.field = f32[512,128]{1,0:T(8,128)S(1)} collective-permute-done((f32[512,128]{1,0:T(8,128)S(1)}, f32[512,128]{1,0:T(8,128)S(1)}, u32[]{:S(2)}, u32[]{:S(2)}) %collective-permute-start.7) | collective-permute-done | bytes 262176 | tf_op jit(solution)/shard_map/ppermute | solution.py:201
  117.8 2.8 %all-to-all-done.4.arrived = bf16[16,128,128]{2,1,0:T(8,128)(2,1)S(1)} async-done(((bf16[16,128,128]{2,1,0:T(8,128)(2,1)}), bf16[16,128,128]{2,1,0:T(8,128)(2,1)S(1)}, u32[]{:S(2)}, u32[]{:S(2)}) %all-to-all-start.4) | async-done | bytes 524320 | tf_op jit(solution)/shard_map/all_to_all | solution.py:230
  120.6 1.4 %shard_map.102 = f32[512,128]{1,0:T(8,128)} custom-call(bf16[512,2048]{1,0:T(8,128)(2,1)S(1)} %get-tuple-element.21.refs_0_.high, bf16[16,128,128]{2,1,0:T(8,128)(2,1)S(1)} %all-to-all-done.4.arrived, f32[512,128]{1,0:T(8,128)S(1)} %collective-permute-done.7.field), custom_call_target="tpu_custom_call" | custom-call | flops 536870912 | bytes 4718592 | tf_op jit(solution)/shard_map/pallas_call | solution.py:26
  (13 shorter events, 5.5 us)
Async XLA Ops:
  0.6 23.9 %copy-start = (f32[1,512,128]{2,1,0:T(8,128)S(1)}, f32[1,512,128]{2,1,0:T(8,128)}, u32[]{:S(2)}) copy-start(f32[1,512,128]{2,1,0:T(8,128)} %param.8) | copy-start | bytes 786436
  2.6 10.8 %collective-permute-start = (f32[512,128]{1,0:T(8,128)S(1)}, f32[512,128]{1,0:T(8,128)S(1)}, u32[]{:S(2)}, u32[]{:S(2)}) collective-permute-start(f32[512,128]{1,0:T(8,128)S(1)} %get-tuple-element.23.refs_1_), channel_id=1, source_target_pairs={{0,16},{1,17},{2,18},{3,19},{4,20},{5,21},{6,22},{7,23},{8,24},{9,... | collective-permute-start | bytes 786440 | tf_op jit(solution)/shard_map/ppermute | solution.py:212
  7.5 12.3 %all-to-all-start = ((s32[16,1,128]{2,1,0:T(1,128)}), s32[16,1,128]{2,1,0:T(1,128)S(1)}, u32[]{:S(2)}, u32[]{:S(2)}) async-start(s32[16,1,128]{2,1,0:T(1,128)} %get-tuple-element.20), calls=%async_computation | async-start | bytes 16384 | tf_op jit(solution)/shard_map/all_to_all | solution.py:230
  20.9 18.0 %all-to-all-start.1 = ((bf16[16,128,128]{2,1,0:T(8,128)(2,1)}), bf16[16,128,128]{2,1,0:T(8,128)(2,1)S(1)}, u32[]{:S(2)}, u32[]{:S(2)}) async-start(bf16[16,128,128]{2,1,0:T(8,128)(2,1)} %get-tuple-element.24), calls=%async_computation.1 | async-start | bytes 1048576 | tf_op jit(solution)/shard_map/all_to_all | solution.py:230
  24.5 10.4 %collective-permute-start.1 = (f32[512,128]{1,0:T(8,128)S(1)}, f32[512,128]{1,0:T(8,128)S(1)}, u32[]{:S(2)}, u32[]{:S(2)}) collective-permute-start(f32[512,128]{1,0:T(8,128)S(1)} %bitcast.4), channel_id=1, source_target_pairs={{16,0},{17,1},{18,2},{19,3},{20,4},{21,5},{22,6},{23,7},{24,8},{25... | collective-permute-start | bytes 786440 | tf_op jit(solution)/shard_map/ppermute | solution.py:201
  42.4 4.5 %collective-permute-start.2 = (bf16[512,128]{1,0:T(8,128)(2,1)S(1)}, bf16[512,128]{1,0:T(8,128)(2,1)S(1)}, u32[]{:S(2)}, u32[]{:S(2)}) collective-permute-start(bf16[512,128]{1,0:T(8,128)(2,1)S(1)} %shard_map.90.after.refs_1_), channel_id=1, source_target_pairs={{0,16},{1,17},{2,18},{3,19},{4,20},{5,21},{6,22},{7,23},{8,24},{9,... | collective-permute-start | bytes 393224 | tf_op jit(solution)/shard_map/ppermute | solution.py:212
  47.0 18.8 %all-to-all-start.2 = ((bf16[16,128,128]{2,1,0:T(8,128)(2,1)}), bf16[16,128,128]{2,1,0:T(8,128)(2,1)S(1)}, u32[]{:S(2)}, u32[]{:S(2)}) async-start(bf16[16,128,128]{2,1,0:T(8,128)(2,1)} %get-tuple-element.28), calls=%async_computation.2 | async-start | bytes 1048576 | tf_op jit(solution)/shard_map/all_to_all | solution.py:230
  51.4 11.6 %collective-permute-start.3 = (f32[512,128]{1,0:T(8,128)S(1)}, f32[512,128]{1,0:T(8,128)S(1)}, u32[]{:S(2)}, u32[]{:S(2)}) collective-permute-start(f32[512,128]{1,0:T(8,128)S(1)} %shard_map.91.refs_2_), channel_id=1, source_target_pairs={{16,0},{17,1},{18,2},{19,3},{20,4},{21,5},{22,6},{23,7},{24,8},{25... | collective-permute-start | bytes 786440 | tf_op jit(solution)/shard_map/ppermute | solution.py:201
  69.3 4.9 %collective-permute-start.4 = (bf16[512,128]{1,0:T(8,128)(2,1)S(1)}, bf16[512,128]{1,0:T(8,128)(2,1)S(1)}, u32[]{:S(2)}, u32[]{:S(2)}) collective-permute-start(bf16[512,128]{1,0:T(8,128)(2,1)S(1)} %shard_map.94.after.refs_1_), channel_id=1, source_target_pairs={{0,16},{1,17},{2,18},{3,19},{4,20},{5,21},{6,22},{7,23},{8,24},{9,... | collective-permute-start | bytes 393224 | tf_op jit(solution)/shard_map/ppermute | solution.py:212
  74.4 18.9 %all-to-all-start.3 = ((bf16[16,128,128]{2,1,0:T(8,128)(2,1)}), bf16[16,128,128]{2,1,0:T(8,128)(2,1)S(1)}, u32[]{:S(2)}, u32[]{:S(2)}) async-start(bf16[16,128,128]{2,1,0:T(8,128)(2,1)} %get-tuple-element.32), calls=%async_computation.3 | async-start | bytes 1048576 | tf_op jit(solution)/shard_map/all_to_all | solution.py:230
  78.8 11.6 %collective-permute-start.5 = (f32[512,128]{1,0:T(8,128)S(1)}, f32[512,128]{1,0:T(8,128)S(1)}, u32[]{:S(2)}, u32[]{:S(2)}) collective-permute-start(f32[512,128]{1,0:T(8,128)S(1)} %shard_map.95.refs_2_), channel_id=1, source_target_pairs={{16,0},{17,1},{18,2},{19,3},{20,4},{21,5},{22,6},{23,7},{24,8},{25... | collective-permute-start | bytes 786440 | tf_op jit(solution)/shard_map/ppermute | solution.py:201
  96.7 4.9 %collective-permute-start.6 = (bf16[512,128]{1,0:T(8,128)(2,1)S(1)}, bf16[512,128]{1,0:T(8,128)(2,1)S(1)}, u32[]{:S(2)}, u32[]{:S(2)}) collective-permute-start(bf16[512,128]{1,0:T(8,128)(2,1)S(1)} %shard_map.98.after.refs_1_), channel_id=1, source_target_pairs={{0,16},{1,17},{2,18},{3,19},{4,20},{5,21},{6,22},{7,23},{8,24},{9,... | collective-permute-start | bytes 393224 | tf_op jit(solution)/shard_map/ppermute | solution.py:212
  101.8 18.9 %all-to-all-start.4 = ((bf16[16,128,128]{2,1,0:T(8,128)(2,1)}), bf16[16,128,128]{2,1,0:T(8,128)(2,1)S(1)}, u32[]{:S(2)}, u32[]{:S(2)}) async-start(bf16[16,128,128]{2,1,0:T(8,128)(2,1)} %get-tuple-element.37), calls=%async_computation.4 | async-start | bytes 1048576 | tf_op jit(solution)/shard_map/all_to_all | solution.py:230
  106.2 11.6 %collective-permute-start.7 = (f32[512,128]{1,0:T(8,128)S(1)}, f32[512,128]{1,0:T(8,128)S(1)}, u32[]{:S(2)}, u32[]{:S(2)}) collective-permute-start(f32[512,128]{1,0:T(8,128)S(1)} %shard_map.99.refs_2_), channel_id=1, source_target_pairs={{16,0},{17,1},{18,2},{19,3},{20,4},{21,5},{22,6},{23,7},{24,8},{25... | collective-permute-start | bytes 786440 | tf_op jit(solution)/shard_map/ppermute | solution.py:201

commit v3 on v2

--- a/solution.py
+++ b/solution.py
@@ -5,7 +5,7 @@
 from jax.experimental.pallas import tpu as pltpu
 from jax.sharding import PartitionSpec as P
 
-VMEM, HBM, ANY = pltpu.VMEM, pltpu.HBM, pl.ANY
+VMEM, SMEM, HBM = pltpu.VMEM, pltpu.SMEM, pltpu.HBM
 DMA = pltpu.SemaphoreType.DMA
 MIB = 1 << 20
 
@@ -60,7 +60,21 @@
 
 
 def panel_kernel(
-    per_patch, rows_hbm, sources_hbm, owner_hbm, retarded, high, low_hbm, rows, sources, owner_map, parts, low, sems
+    per_patch,
+    rows_hbm,
+    sources_hbm,
+    owner_hbm,
+    retarded,
+    inverse_hbm,
+    high,
+    low_hbm,
+    inverse,
+    rows,
+    sources,
+    owner_map,
+    parts,
+    low,
+    sems,
 ):
     size = retarded.shape[-1]
     slots, chunk = parts.shape[:2]
@@ -74,6 +88,7 @@
         (rows_hbm, rows, sems.at[slots]),
         (sources_hbm, sources, sems.at[slots + 1]),
         (owner_hbm, owner_map, sems.at[slots + 2]),
+        (inverse_hbm, inverse, sems.at[slots + 3]),
     )
     for c in range(min(slots, chunks)):
         fetch(c).start()
@@ -94,7 +109,9 @@
             rounded = block.astype(high.dtype)
             rest = (block - rounded.astype(jnp.float32)).astype(low.dtype)
             high[pl.ds(row, size), pl.ds(column, size)] = rounded
-            low[pl.ds(row, size), pl.ds(column, size)] = rest
+            piece = column // low.shape[2]
+            inside = pl.multiple_of(column - piece * low.shape[2], size)
+            low[piece, pl.ds(row, size), pl.ds(inside, size)] = rest
 
         return carry
 
@@ -120,13 +137,17 @@
     return jnp.concatenate(parts, axis=0).astype(jnp.bfloat16)
 
 
-def product(high, low_hbm, arrived, low, sem):
+def product(high, low_hbm, arrived, low, sems):
     patches, size, columns = arrived.shape
-    (copy,) = started((low_hbm, low, sem))
+    pieces, _, depth = low.shape
+    copies = started(*((low_hbm.at[k], low.at[k], sems.at[k]) for k in range(pieces)))
     flat = arrived[...].reshape(patches * size, columns)
     fresh = jnp.dot(high[...], flat, preferred_element_type=jnp.float32)
-    copy.wait()
-    return fresh + jnp.dot(low[...], flat, preferred_element_type=jnp.float32)
+    for k, copy in enumerate(copies):
+        copy.wait()
+        here = flat[k * depth : (k + 1) * depth]
+        fresh = fresh + jnp.dot(low[k], here, preferred_element_type=jnp.float32)
+    return fresh
 
 
 def first_kernel(keeps, incident_hbm, own, received, inverse_hbm, current, incident, inverse, sems):
@@ -140,29 +161,37 @@
     current[...] = solved(incident[...].astype(jnp.float32) - field, inverse)
 
 
-def solve_kernel(
-    step, high, low_hbm, arrived, field, incident_hbm, inverse_hbm, current, low, incident, inverse, sems
-):
+def stage_kernel(step, incident_hbm, field, staged, incident, sem):
+    first = lax.axis_index("lag") == 0
+
+    @pl.when(first)
+    def _():
+        started((incident_hbm.at[step], incident, sem))[0].wait()
+        staged[...] = incident[...].astype(jnp.float32) - field[...]
+
+    @pl.when(jnp.logical_not(first))
+    def _():
+        staged[...] = field[...]
+
+
+def solve_kernel(high, low_hbm, arrived, staged, inverse, current, low, sems):
     @pl.when(lax.axis_index("lag") == 0)
     def _():
-        copies = started(
-            (incident_hbm.at[step], incident, sems.at[0]),
-            (inverse_hbm, inverse, sems.at[1]),
-        )
-        fresh = product(high, low_hbm, arrived, low, sems.at[2])
-        for copy in copies:
-            copy.wait()
-        excess = incident[...].astype(jnp.float32) - (field[...] + fresh)
-        current[...] = solved(excess, inverse)
-
-
-def partial_kernel(high, low_hbm, arrived, field, after, partial, low, sem):
+        current[...] = solved(staged[...] - product(high, low_hbm, arrived, low, sems), inverse)
+
+
+def partial_kernel(high, low_hbm, arrived, staged, after, partial, low, sems):
     del after
 
     @pl.when(lax.axis_index("lag") > 0)
     def _():
-        fresh = product(high, low_hbm, arrived, low, sem)
-        partial[...] = field[...] + fresh
+        partial[...] = staged[...] + product(high, low_hbm, arrived, low, sems)
+
+
+def asked_kernel(table, asked, copy_of, sem):
+    started((table, copy_of, sem))[0].wait()
+    for q in range(table.shape[0]):
+        asked[q] = jnp.maximum(copy_of[q, 0, 0], 0)
 
 
 def ahead_kernel(high, arrived, field, ahead_hbm, ahead, sems):
@@ -188,8 +217,7 @@
     def _():
         copies = []
         for q in range(patches):
-            block = jnp.max(jnp.maximum(asked[q], 0))
-            start = pl.multiple_of(block * size, size)
+            start = pl.multiple_of(asked[q] * size, size)
             copies.append((current.at[pl.ds(start, size)], outgoing.at[q], sems.at[q]))
         copies.append((current, currents.at[step], sems.at[patches]))
         for copy in started(*copies):
@@ -238,7 +266,7 @@
         return call(
             lambda *refs: pack_kernel(step, keeps, early, *refs),
             [(HBM, (patches, size, columns), bf16), (HBM, incident.shape, bf16)],
-            [(VMEM, asked), (VMEM, current)] + [(VMEM, x) for x in after] + [(HBM, x) for x in held],
+            [(SMEM, asked), (VMEM, current)] + [(VMEM, x) for x in after] + [(HBM, x) for x in held],
             [DMA((patches + 1,))],
             aliases=aliases,
         )
@@ -254,7 +282,12 @@
             DMA((3,)),
         ],
     )
-    asked = exchange(wanted)
+    asked = call(
+        asked_kernel,
+        [(SMEM, (patches,), jnp.int32)],
+        [(VMEM, exchange(wanted))],
+        [pltpu.SMEM(wanted.shape, jnp.int32), DMA],
+    )
     own, received, keeps = spread(first_field)
     solve_scratch = [pltpu.VMEM(column, bf16), pltpu.VMEM(self_inverse.shape, f32), DMA((3,))]
     current = call(
@@ -266,17 +299,19 @@
     )
     chunk = max(n for n in range(1, 9) if listed % n == 0)
     panel = (unknowns, patches * size)
-    high, low = call(
+    pieces = 4 if patches % 4 == 0 else 1
+    low_panel = (pieces, unknowns, patches * size // pieces)
+    high, low, inverse = call(
         lambda *refs: panel_kernel(per_patch, *refs),
-        [(VMEM, panel, bf16), (HBM, panel, bf16)],
-        [(HBM, block_rows), (HBM, block_sources), (HBM, owner_map), (HBM, retarded)],
+        [(VMEM, panel, bf16), (HBM, low_panel, bf16), (VMEM, self_inverse.shape, f32)],
+        [(HBM, block_rows), (HBM, block_sources), (HBM, owner_map), (HBM, retarded), (HBM, self_inverse)],
         [
             pltpu.SMEM(block_rows.shape, jnp.int32),
             pltpu.SMEM(block_sources.shape, jnp.int32),
             pltpu.SMEM(owner_map.shape, jnp.int32),
             pltpu.VMEM((3, chunk, size, size), f32),
-            pltpu.VMEM(panel, bf16),
-            DMA((6,)),
+            pltpu.VMEM(low_panel, bf16),
+            DMA((7,)),
         ],
         nbytes=listed * size * size * 4 + panel_bytes,
         vmem=panel_bytes // 2,
@@ -293,30 +328,20 @@
         arrived = exchange(outgoing)
         field = shifted(field)
         if step + 1 < steps:
+            staged = call(
+                lambda *refs, n=step + 1: stage_kernel(n, *refs),
+                [(VMEM, column, f32)],
+                [(HBM, incident), (VMEM, field)],
+                [pltpu.VMEM(column, bf16), DMA],
+            )
+            shared = [(VMEM, high), (HBM, low), (VMEM, arrived), (VMEM, staged)]
+            scratch = [pltpu.VMEM(low_panel, bf16), DMA((pieces,))]
+            sizes = [all_flops, panel_bytes + arrived_bytes, panel_bytes + arrived_bytes]
             current = call(
-                lambda *refs, n=step + 1: solve_kernel(n, *refs),
-                [(VMEM, column, bf16)],
-                [
-                    (VMEM, high),
-                    (HBM, low),
-                    (VMEM, arrived),
-                    (VMEM, field),
-                    (HBM, incident),
-                    (HBM, self_inverse),
-                ],
-                [pltpu.VMEM(panel, bf16), *solve_scratch],
-                all_flops + solve_flops,
-                panel_bytes + arrived_bytes,
-                panel_bytes + arrived_bytes,
+                solve_kernel, [(VMEM, column, bf16)], [*shared, (VMEM, inverse)], scratch, *sizes
             )
             field = call(
-                partial_kernel,
-                [(VMEM, column, f32)],
-                [(VMEM, high), (HBM, low), (VMEM, arrived), (VMEM, field), (VMEM, current)],
-                [pltpu.VMEM(panel, bf16), DMA],
-                all_flops,
-                panel_bytes + arrived_bytes,
-                panel_bytes + arrived_bytes,
+                partial_kernel, [(VMEM, column, f32)], [*shared, (VMEM, current)], scratch, *sizes
             )
         else:
             field = call(

time: 124 us -> 125 us (level)
  blocking collectives: 0 us -> 12.3 us
  waiting for transfers between devices: 57.4 us -> 50 us
  starting transfers between devices: 38 us -> 31.4 us
  Pallas kernels: 25.7 us -> 29.1 us
    all_to_all x0 -> x1, blocking collectives: none -> 12.3 us  [exchange(): return lax.all_to_all(x, 'patch', split_axis=0, concat_axis=0, tiled=True)]
    all_to_all x5 -> x4, waiting for transfers between devices: 17.3 us -> 10.3 us  [exchange(): return lax.all_to_all(x, 'patch', split_axis=0, concat_axis=0, tiled=True)]
    all_to_all x5 -> x4, starting transfers between devices: 22.6 us -> 16.7 us  [exchange(): return lax.all_to_all(x, 'patch', split_axis=0, concat_axis=0, tiled=True)]
    pallas_call x17 -> x21, Pallas kernels: 25.7 us -> 29.1 us  [call(): run(*(pltpu.with_memory_space_constraint(x, space) for space, x in ins))]
  transfers between devices with their start and end apart: 13 -> 12, of which waited for: 12 -> 11; matrix products, arithmetic and copies ran while one was open for 0% -> 0% of each run, Pallas kernels for 9% -> 10%
where the time goes in v3:
time: 125 us; the launch traced here: 124 us
  waiting for transfers between devices  50 us (40%)
  starting transfers between devices  31.4 us (25%)
  Pallas kernels  29.1 us (23%)
  blocking collectives  12.3 us (10%)
    ppermute x4, waiting for transfers between devices, shifted(): return lax.ppermute(x, 'lag', [(i, i - 1) for i in range(1, sections)])  34.1 us
    pallas_call x21, Pallas kernels, call(): run(*(pltpu.with_memory_space_constraint(x, space) for space, x in ins))  29.1 us
    all_to_all x4, starting transfers between devices, exchange(): return lax.all_to_all(x, 'patch', split_axis=0, concat_axis=0, tiled=True)  16.7 us
    all_to_all x1, blocking collectives, exchange(): return lax.all_to_all(x, 'patch', split_axis=0, concat_axis=0, tiled=True)  12.3 us
    all_to_all x4, waiting for transfers between devices, exchange(): return lax.all_to_all(x, 'patch', split_axis=0, concat_axis=0, tiled=True)  10.3 us
    ppermute x4, starting transfers between devices, spread(): received = lax.ppermute(x, 'lag', pairs)  9.58 us
    ppermute x4, waiting for transfers between devices, spread(): received = lax.ppermute(x, 'lag', pairs)  5.64 us
    ppermute x4, starting transfers between devices, shifted(): return lax.ppermute(x, 'lag', [(i, i - 1) for i in range(1, sections)])  5.17 us
  transfers between devices with their start and end apart: 12, of which 11 were waited for; matrix products, arithmetic and copies ran while one was open for 0% of the time, Pallas kernels for 10%

profile of v3, /device:TPU:0, one launch (start us, length us, event | category | flops | bytes accessed | tf_op | source)
XLA Modules:
  0.0 123.9 jit_solution(15569611004630483687)
XLA Ops:
  0.6 1.9 %shard_map.86 = (s32[16,1,128]{2,1,0:T(1,128)}, f32[512,128]{1,0:T(8,128)S(1)}) custom-call(s32[1,1,56]{2,1,0:T(1,128)} %refs_1_.3, s32[64]{0:T(128)} %refs_2_.1, f32[512,128]{1,0:T(8,128)} %bitcast.3), custom_call_target="tpu_custom_call" | custom-call | tf_op jit(solution)/shard_map/pallas_call | solution.py:26
  2.6 4.9 %collective-permute-start = (f32[512,128]{1,0:T(8,128)S(1)}, f32[512,128]{1,0:T(8,128)S(1)}, u32[]{:S(2)}, u32[]{:S(2)}) collective-permute-start(f32[512,128]{1,0:T(8,128)S(1)} %get-tuple-element.24.refs_1_), channel_id=1, source_target_pairs={{0,16},{1,17},{2,18},{3,19},{4,20},{5,21},{6,22},{7,23},{8,24},{9,... | collective-permute-start | bytes 786440 | tf_op jit(solution)/shard_map/ppermute | solution.py:240
  7.5 12.3 %all_to_all.25.table = s32[16,1,128]{2,1,0:T(1,128)S(1)} all-to-all(s32[16,1,128]{2,1,0:T(1,128)} %get-tuple-element.21), channel_id=1, replica_groups=mesh['lag'=2,'patch'=16] {'patch'}, dimensions={0} | all-to-all | bytes 16384 | tf_op jit(solution)/shard_map/all_to_all | solution.py:258
  20.4 1.4 %shard_map.89.refs_1_ = bf16[512,128]{1,0:T(8,128)(2,1)S(1)} custom-call(bf16[4,512,128]{2,1,0:T(8,128)(2,1)} %refs_0_.11, f32[512,128]{1,0:T(8,128)S(1)} %get-tuple-element.24.refs_1_, f32[512,128]{1,0:T(8,128)S(1)} %collective-permute-done.refs_2_, f32[4,128,128]{2,1,0:T(8,128)} %refs_3_.3), custom_call_target="tpu_custom_call" | custom-call | flops 100663296 | tf_op jit(solution)/shard_map/pallas_call | solution.py:26
  22.9 3.6 %all-to-all-start.1 = ((bf16[16,128,128]{2,1,0:T(8,128)(2,1)}), bf16[16,128,128]{2,1,0:T(8,128)(2,1)S(1)}, u32[]{:S(2)}, u32[]{:S(2)}) async-start(bf16[16,128,128]{2,1,0:T(8,128)(2,1)} %get-tuple-element.25), calls=%async_computation.1 | async-start | bytes 1048576 | tf_op jit(solution)/shard_map/all_to_all | solution.py:258
  26.5 1.3 %collective-permute-start.1 = (f32[512,128]{1,0:T(8,128)S(1)}, f32[512,128]{1,0:T(8,128)S(1)}, u32[]{:S(2)}, u32[]{:S(2)}) collective-permute-start(f32[512,128]{1,0:T(8,128)S(1)} %bitcast.4), channel_id=1, source_target_pairs={{16,0},{17,1},{18,2},{19,3},{20,4},{21,5},{22,6},{23,7},{24,8},{25... | collective-permute-start | bytes 786440 | tf_op jit(solution)/shard_map/ppermute | solution.py:229
  27.8 5.4 %shard_map.88 = (bf16[512,2048]{1,0:T(8,128)(2,1)S(1)}, bf16[4,512,512]{2,1,0:T(8,128)(2,1)}, f32[4,128,128]{2,1,0:T(8,128)S(1)}) custom-call(s32[1,1,56]{2,1,0:T(1,128)} %refs_0_.7, s32[1,1,56]{2,1,0:T(1,128)} %refs_1_.3, s32[64]{0:T(128)} %refs_2_.1, f32[1,1,56,128,128]{4,3,2,1,0:T(8,128)} %refs_3_.2, f32[4,128,128]{2,1,0:T(8,128)} %refs_3_.3), custom_call_target="tpu_custom_call" | custom-call | bytes 7864320 | tf_op jit(solution)/shard_map/pallas_call | solution.py:26
  33.2 3.6 %collective-permute-done.1.refs_1_ = f32[512,128]{1,0:T(8,128)S(1)} collective-permute-done((f32[512,128]{1,0:T(8,128)S(1)}, f32[512,128]{1,0:T(8,128)S(1)}, u32[]{:S(2)}, u32[]{:S(2)}) %collective-permute-start.1) | collective-permute-done | bytes 262176 | tf_op jit(solution)/shard_map/ppermute | solution.py:229
  37.8 3.1 %all-to-all-done.1.arrived = bf16[16,128,128]{2,1,0:T(8,128)(2,1)S(1)} async-done(((bf16[16,128,128]{2,1,0:T(8,128)(2,1)}), bf16[16,128,128]{2,1,0:T(8,128)(2,1)S(1)}, u32[]{:S(2)}, u32[]{:S(2)}) %all-to-all-start.1) | async-done | bytes 524320 | tf_op jit(solution)/shard_map/all_to_all | solution.py:258
  40.9 3.6 %shard_map.92.after.refs_1_ = bf16[512,128]{1,0:T(8,128)(2,1)S(1)} custom-call(bf16[512,2048]{1,0:T(8,128)(2,1)S(1)} %get-tuple-element.22.high, bf16[4,512,512]{2,1,0:T(8,128)(2,1)} %get-tuple-element.23.low_hbm, bf16[16,128,128]{2,1,0:T(8,128)(2,1)S(1)} %all-to-all-done.1.arrived, f32[512,128]{1,0:T(8,128)S(1)} %shard_map.91.staged, ...), custom_call_target="tpu_custom_call" | custom-call | flops 536870912 | bytes 4718592 | tf_op jit(solution)/shard_map/pallas_call | solution.py:26
  44.5 1.3 %collective-permute-start.2 = (bf16[512,128]{1,0:T(8,128)(2,1)S(1)}, bf16[512,128]{1,0:T(8,128)(2,1)S(1)}, u32[]{:S(2)}, u32[]{:S(2)}) collective-permute-start(bf16[512,128]{1,0:T(8,128)(2,1)S(1)} %shard_map.92.after.refs_1_), channel_id=1, source_target_pairs={{0,16},{1,17},{2,18},{3,19},{4,20},{5,21},{6,22},{7,23},{8,24},{9,... | collective-permute-start | bytes 393224 | tf_op jit(solution)/shard_map/ppermute | solution.py:240
  45.8 1.0 shard_map.94
  46.8 2.1 %collective-permute-done.2.refs_1_ = bf16[512,128]{1,0:T(8,128)(2,1)S(1)} collective-permute-done((bf16[512,128]{1,0:T(8,128)(2,1)S(1)}, bf16[512,128]{1,0:T(8,128)(2,1)S(1)}, u32[]{:S(2)}, u32[]{:S(2)}) %collective-permute-start.2) | collective-permute-done | bytes 131104 | tf_op jit(solution)/shard_map/ppermute | solution.py:240
  49.1 4.3 %all-to-all-start.2 = ((bf16[16,128,128]{2,1,0:T(8,128)(2,1)}), bf16[16,128,128]{2,1,0:T(8,128)(2,1)S(1)}, u32[]{:S(2)}, u32[]{:S(2)}) async-start(bf16[16,128,128]{2,1,0:T(8,128)(2,1)} %get-tuple-element.30), calls=%async_computation.2 | async-start | bytes 1048576 | tf_op jit(solution)/shard_map/all_to_all | solution.py:258
  53.4 1.3 %collective-permute-start.3 = (f32[512,128]{1,0:T(8,128)S(1)}, f32[512,128]{1,0:T(8,128)S(1)}, u32[]{:S(2)}, u32[]{:S(2)}) collective-permute-start(f32[512,128]{1,0:T(8,128)S(1)} %shard_map.93.refs_2_), channel_id=1, source_target_pairs={{16,0},{17,1},{18,2},{19,3},{20,4},{21,5},{22,6},{23,7},{24,8},{25... | collective-permute-start | bytes 786440 | tf_op jit(solution)/shard_map/ppermute | solution.py:229
  54.7 10.1 %collective-permute-done.3.refs_1_ = f32[512,128]{1,0:T(8,128)S(1)} collective-permute-done((f32[512,128]{1,0:T(8,128)S(1)}, f32[512,128]{1,0:T(8,128)S(1)}, u32[]{:S(2)}, u32[]{:S(2)}) %collective-permute-start.3) | collective-permute-done | bytes 262176 | tf_op jit(solution)/shard_map/ppermute | solution.py:229
  65.8 2.1 %all-to-all-done.2.arrived = bf16[16,128,128]{2,1,0:T(8,128)(2,1)S(1)} async-done(((bf16[16,128,128]{2,1,0:T(8,128)(2,1)}), bf16[16,128,128]{2,1,0:T(8,128)(2,1)S(1)}, u32[]{:S(2)}, u32[]{:S(2)}) %all-to-all-start.2) | async-done | bytes 524320 | tf_op jit(solution)/shard_map/all_to_all | solution.py:258
  67.9 3.6 %shard_map.97.after.refs_1_ = bf16[512,128]{1,0:T(8,128)(2,1)S(1)} custom-call(bf16[512,2048]{1,0:T(8,128)(2,1)S(1)} %get-tuple-element.22.high, bf16[4,512,512]{2,1,0:T(8,128)(2,1)} %get-tuple-element.23.low_hbm, bf16[16,128,128]{2,1,0:T(8,128)(2,1)S(1)} %all-to-all-done.2.arrived, f32[512,128]{1,0:T(8,128)S(1)} %shard_map.96.staged, ...), custom_call_target="tpu_custom_call" | custom-call | flops 536870912 | bytes 4718592 | tf_op jit(solution)/shard_map/pallas_call | solution.py:26
  71.5 1.7 %collective-permute-start.4 = (bf16[512,128]{1,0:T(8,128)(2,1)S(1)}, bf16[512,128]{1,0:T(8,128)(2,1)S(1)}, u32[]{:S(2)}, u32[]{:S(2)}) collective-permute-start(bf16[512,128]{1,0:T(8,128)(2,1)S(1)} %shard_map.97.after.refs_1_), channel_id=1, source_target_pairs={{0,16},{1,17},{2,18},{3,19},{4,20},{5,21},{6,22},{7,23},{8,24},{9,... | collective-permute-start | bytes 393224 | tf_op jit(solution)/shard_map/ppermute | solution.py:240
  74.2 1.8 %collective-permute-done.4.refs_1_ = bf16[512,128]{1,0:T(8,128)(2,1)S(1)} collective-permute-done((bf16[512,128]{1,0:T(8,128)(2,1)S(1)}, bf16[512,128]{1,0:T(8,128)(2,1)S(1)}, u32[]{:S(2)}, u32[]{:S(2)}) %collective-permute-start.4) | collective-permute-done | bytes 131104 | tf_op jit(solution)/shard_map/ppermute | solution.py:240
  76.2 4.4 %all-to-all-start.3 = ((bf16[16,128,128]{2,1,0:T(8,128)(2,1)}), bf16[16,128,128]{2,1,0:T(8,128)(2,1)S(1)}, u32[]{:S(2)}, u32[]{:S(2)}) async-start(bf16[16,128,128]{2,1,0:T(8,128)(2,1)} %get-tuple-element.34), calls=%async_computation.3 | async-start | bytes 1048576 | tf_op jit(solution)/shard_map/all_to_all | solution.py:258
  80.6 1.3 %collective-permute-start.5 = (f32[512,128]{1,0:T(8,128)S(1)}, f32[512,128]{1,0:T(8,128)S(1)}, u32[]{:S(2)}, u32[]{:S(2)}) collective-permute-start(f32[512,128]{1,0:T(8,128)S(1)} %shard_map.98.refs_2_), channel_id=1, source_target_pairs={{16,0},{17,1},{18,2},{19,3},{20,4},{21,5},{22,6},{23,7},{24,8},{25... | collective-permute-start | bytes 786440 | tf_op jit(solution)/shard_map/ppermute | solution.py:229
  81.9 10.1 %collective-permute-done.5.refs_1_ = f32[512,128]{1,0:T(8,128)S(1)} collective-permute-done((f32[512,128]{1,0:T(8,128)S(1)}, f32[512,128]{1,0:T(8,128)S(1)}, u32[]{:S(2)}, u32[]{:S(2)}) %collective-permute-start.5) | collective-permute-done | bytes 262176 | tf_op jit(solution)/shard_map/ppermute | solution.py:229
  93.0 2.1 %all-to-all-done.3.arrived = bf16[16,128,128]{2,1,0:T(8,128)(2,1)S(1)} async-done(((bf16[16,128,128]{2,1,0:T(8,128)(2,1)}), bf16[16,128,128]{2,1,0:T(8,128)(2,1)S(1)}, u32[]{:S(2)}, u32[]{:S(2)}) %all-to-all-start.3) | async-done | bytes 524320 | tf_op jit(solution)/shard_map/all_to_all | solution.py:258
  95.1 3.6 %shard_map.102.after.refs_1_ = bf16[512,128]{1,0:T(8,128)(2,1)S(1)} custom-call(bf16[512,2048]{1,0:T(8,128)(2,1)S(1)} %get-tuple-element.22.high, bf16[4,512,512]{2,1,0:T(8,128)(2,1)} %get-tuple-element.23.low_hbm, bf16[16,128,128]{2,1,0:T(8,128)(2,1)S(1)} %all-to-all-done.3.arrived, f32[512,128]{1,0:T(8,128)S(1)} %shard_map.101.staged, ...), custom_call_target="tpu_custom_call" | custom-call | flops 536870912 | bytes 4718592 | tf_op jit(solution)/shard_map/pallas_call | solution.py:26
  98.7 1.7 %collective-permute-start.6 = (bf16[512,128]{1,0:T(8,128)(2,1)S(1)}, bf16[512,128]{1,0:T(8,128)(2,1)S(1)}, u32[]{:S(2)}, u32[]{:S(2)}) collective-permute-start(bf16[512,128]{1,0:T(8,128)(2,1)S(1)} %shard_map.102.after.refs_1_), channel_id=1, source_target_pairs={{0,16},{1,17},{2,18},{3,19},{4,20},{5,21},{6,22},{7,23},{8,24},{9,... | collective-permute-start | bytes 393224 | tf_op jit(solution)/shard_map/ppermute | solution.py:240
  101.6 1.7 %collective-permute-done.6.refs_1_ = bf16[512,128]{1,0:T(8,128)(2,1)S(1)} collective-permute-done((bf16[512,128]{1,0:T(8,128)(2,1)S(1)}, bf16[512,128]{1,0:T(8,128)(2,1)S(1)}, u32[]{:S(2)}, u32[]{:S(2)}) %collective-permute-start.6) | collective-permute-done | bytes 131104 | tf_op jit(solution)/shard_map/ppermute | solution.py:240
  103.5 4.4 %all-to-all-start.4 = ((bf16[16,128,128]{2,1,0:T(8,128)(2,1)}), bf16[16,128,128]{2,1,0:T(8,128)(2,1)S(1)}, u32[]{:S(2)}, u32[]{:S(2)}) async-start(bf16[16,128,128]{2,1,0:T(8,128)(2,1)} %get-tuple-element.39), calls=%async_computation.4 | async-start | bytes 1048576 | tf_op jit(solution)/shard_map/all_to_all | solution.py:258
  107.9 1.3 %collective-permute-start.7 = (f32[512,128]{1,0:T(8,128)S(1)}, f32[512,128]{1,0:T(8,128)S(1)}, u32[]{:S(2)}, u32[]{:S(2)}) collective-permute-start(f32[512,128]{1,0:T(8,128)S(1)} %shard_map.103.refs_2_), channel_id=1, source_target_pairs={{16,0},{17,1},{18,2},{19,3},{20,4},{21,5},{22,6},{23,7},{24,8},{25... | collective-permute-start | bytes 786440 | tf_op jit(solution)/shard_map/ppermute | solution.py:229
  109.2 10.1 %collective-permute-done.7.field = f32[512,128]{1,0:T(8,128)S(1)} collective-permute-done((f32[512,128]{1,0:T(8,128)S(1)}, f32[512,128]{1,0:T(8,128)S(1)}, u32[]{:S(2)}, u32[]{:S(2)}) %collective-permute-start.7) | collective-permute-done | bytes 262176 | tf_op jit(solution)/shard_map/ppermute | solution.py:229
  119.3 3.0 %all-to-all-done.4.arrived = bf16[16,128,128]{2,1,0:T(8,128)(2,1)S(1)} async-done(((bf16[16,128,128]{2,1,0:T(8,128)(2,1)}), bf16[16,128,128]{2,1,0:T(8,128)(2,1)S(1)}, u32[]{:S(2)}, u32[]{:S(2)}) %all-to-all-start.4) | async-done | bytes 524320 | tf_op jit(solution)/shard_map/all_to_all | solution.py:258
  122.3 1.4 %shard_map.106 = f32[512,128]{1,0:T(8,128)} custom-call(bf16[512,2048]{1,0:T(8,128)(2,1)S(1)} %get-tuple-element.22.high, bf16[16,128,128]{2,1,0:T(8,128)(2,1)S(1)} %all-to-all-done.4.arrived, f32[512,128]{1,0:T(8,128)S(1)} %collective-permute-done.7.field), custom_call_target="tpu_custom_call" | custom-call | flops 536870912 | bytes 4718592 | tf_op jit(solution)/shard_map/pallas_call | solution.py:26
  (16 shorter events, 7.3 us)
Async XLA Ops:
  0.6 25.8 %copy-start = (f32[1,512,128]{2,1,0:T(8,128)S(1)}, f32[1,512,128]{2,1,0:T(8,128)}, u32[]{:S(2)}) copy-start(f32[1,512,128]{2,1,0:T(8,128)} %param.8) | copy-start | bytes 786436
  2.6 17.9 %collective-permute-start = (f32[512,128]{1,0:T(8,128)S(1)}, f32[512,128]{1,0:T(8,128)S(1)}, u32[]{:S(2)}, u32[]{:S(2)}) collective-permute-start(f32[512,128]{1,0:T(8,128)S(1)} %get-tuple-element.24.refs_1_), channel_id=1, source_target_pairs={{0,16},{1,17},{2,18},{3,19},{4,20},{5,21},{6,22},{7,23},{8,24},{9,... | collective-permute-start | bytes 786440 | tf_op jit(solution)/shard_map/ppermute | solution.py:240
  22.9 18.0 %all-to-all-start.1 = ((bf16[16,128,128]{2,1,0:T(8,128)(2,1)}), bf16[16,128,128]{2,1,0:T(8,128)(2,1)S(1)}, u32[]{:S(2)}, u32[]{:S(2)}) async-start(bf16[16,128,128]{2,1,0:T(8,128)(2,1)} %get-tuple-element.25), calls=%async_computation.1 | async-start | bytes 1048576 | tf_op jit(solution)/shard_map/all_to_all | solution.py:258
  26.5 10.4 %collective-permute-start.1 = (f32[512,128]{1,0:T(8,128)S(1)}, f32[512,128]{1,0:T(8,128)S(1)}, u32[]{:S(2)}, u32[]{:S(2)}) collective-permute-start(f32[512,128]{1,0:T(8,128)S(1)} %bitcast.4), channel_id=1, source_target_pairs={{16,0},{17,1},{18,2},{19,3},{20,4},{21,5},{22,6},{23,7},{24,8},{25... | collective-permute-start | bytes 786440 | tf_op jit(solution)/shard_map/ppermute | solution.py:229
  44.5 4.5 %collective-permute-start.2 = (bf16[512,128]{1,0:T(8,128)(2,1)S(1)}, bf16[512,128]{1,0:T(8,128)(2,1)S(1)}, u32[]{:S(2)}, u32[]{:S(2)}) collective-permute-start(bf16[512,128]{1,0:T(8,128)(2,1)S(1)} %shard_map.92.after.refs_1_), channel_id=1, source_target_pairs={{0,16},{1,17},{2,18},{3,19},{4,20},{5,21},{6,22},{7,23},{8,24},{9,... | collective-permute-start | bytes 393224 | tf_op jit(solution)/shard_map/ppermute | solution.py:240
  49.1 18.8 %all-to-all-start.2 = ((bf16[16,128,128]{2,1,0:T(8,128)(2,1)}), bf16[16,128,128]{2,1,0:T(8,128)(2,1)S(1)}, u32[]{:S(2)}, u32[]{:S(2)}) async-start(bf16[16,128,128]{2,1,0:T(8,128)(2,1)} %get-tuple-element.30), calls=%async_computation.2 | async-start | bytes 1048576 | tf_op jit(solution)/shard_map/all_to_all | solution.py:258
  53.4 11.4 %collective-permute-start.3 = (f32[512,128]{1,0:T(8,128)S(1)}, f32[512,128]{1,0:T(8,128)S(1)}, u32[]{:S(2)}, u32[]{:S(2)}) collective-permute-start(f32[512,128]{1,0:T(8,128)S(1)} %shard_map.93.refs_2_), channel_id=1, source_target_pairs={{16,0},{17,1},{18,2},{19,3},{20,4},{21,5},{22,6},{23,7},{24,8},{25... | collective-permute-start | bytes 786440 | tf_op jit(solution)/shard_map/ppermute | solution.py:229
  71.5 4.6 %collective-permute-start.4 = (bf16[512,128]{1,0:T(8,128)(2,1)S(1)}, bf16[512,128]{1,0:T(8,128)(2,1)S(1)}, u32[]{:S(2)}, u32[]{:S(2)}) collective-permute-start(bf16[512,128]{1,0:T(8,128)(2,1)S(1)} %shard_map.97.after.refs_1_), channel_id=1, source_target_pairs={{0,16},{1,17},{2,18},{3,19},{4,20},{5,21},{6,22},{7,23},{8,24},{9,... | collective-permute-start | bytes 393224 | tf_op jit(solution)/shard_map/ppermute | solution.py:240
  76.2 18.9 %all-to-all-start.3 = ((bf16[16,128,128]{2,1,0:T(8,128)(2,1)}), bf16[16,128,128]{2,1,0:T(8,128)(2,1)S(1)}, u32[]{:S(2)}, u32[]{:S(2)}) async-start(bf16[16,128,128]{2,1,0:T(8,128)(2,1)} %get-tuple-element.34), calls=%async_computation.3 | async-start | bytes 1048576 | tf_op jit(solution)/shard_map/all_to_all | solution.py:258
  80.6 11.4 %collective-permute-start.5 = (f32[512,128]{1,0:T(8,128)S(1)}, f32[512,128]{1,0:T(8,128)S(1)}, u32[]{:S(2)}, u32[]{:S(2)}) collective-permute-start(f32[512,128]{1,0:T(8,128)S(1)} %shard_map.98.refs_2_), channel_id=1, source_target_pairs={{16,0},{17,1},{18,2},{19,3},{20,4},{21,5},{22,6},{23,7},{24,8},{25... | collective-permute-start | bytes 786440 | tf_op jit(solution)/shard_map/ppermute | solution.py:229
  98.7 4.6 %collective-permute-start.6 = (bf16[512,128]{1,0:T(8,128)(2,1)S(1)}, bf16[512,128]{1,0:T(8,128)(2,1)S(1)}, u32[]{:S(2)}, u32[]{:S(2)}) collective-permute-start(bf16[512,128]{1,0:T(8,128)(2,1)S(1)} %shard_map.102.after.refs_1_), channel_id=1, source_target_pairs={{0,16},{1,17},{2,18},{3,19},{4,20},{5,21},{6,22},{7,23},{8,24},{9,... | collective-permute-start | bytes 393224 | tf_op jit(solution)/shard_map/ppermute | solution.py:240
  103.5 18.9 %all-to-all-start.4 = ((bf16[16,128,128]{2,1,0:T(8,128)(2,1)}), bf16[16,128,128]{2,1,0:T(8,128)(2,1)S(1)}, u32[]{:S(2)}, u32[]{:S(2)}) async-start(bf16[16,128,128]{2,1,0:T(8,128)(2,1)} %get-tuple-element.39), calls=%async_computation.4 | async-start | bytes 1048576 | tf_op jit(solution)/shard_map/all_to_all | solution.py:258
  107.9 11.4 %collective-permute-start.7 = (f32[512,128]{1,0:T(8,128)S(1)}, f32[512,128]{1,0:T(8,128)S(1)}, u32[]{:S(2)}, u32[]{:S(2)}) collective-permute-start(f32[512,128]{1,0:T(8,128)S(1)} %shard_map.103.refs_2_), channel_id=1, source_target_pairs={{16,0},{17,1},{18,2},{19,3},{20,4},{21,5},{22,6},{23,7},{24,8},{25... | collective-permute-start | bytes 786440 | tf_op jit(solution)/shard_map/ppermute | solution.py:229

commit v4 on v3

--- a/solution.py
+++ b/solution.py
@@ -137,17 +137,31 @@
     return jnp.concatenate(parts, axis=0).astype(jnp.bfloat16)
 
 
-def product(high, low_hbm, arrived, low, sems):
+def product(here, high, low_hbm, arrived, low, total, sems, finish):
     patches, size, columns = arrived.shape
     pieces, _, depth = low.shape
-    copies = started(*((low_hbm.at[k], low.at[k], sems.at[k]) for k in range(pieces)))
-    flat = arrived[...].reshape(patches * size, columns)
-    fresh = jnp.dot(high[...], flat, preferred_element_type=jnp.float32)
-    for k, copy in enumerate(copies):
-        copy.wait()
-        here = flat[k * depth : (k + 1) * depth]
-        fresh = fresh + jnp.dot(low[k], here, preferred_element_type=jnp.float32)
-    return fresh
+    copies = [pltpu.make_async_copy(low_hbm.at[k], low.at[k], sems.at[k]) for k in range(pieces)]
+
+    @pl.when(here)
+    def _():
+        for copy in copies:
+            copy.start()
+        rows = total.shape[0] // 2
+
+        def half(part, carry):
+            flat = arrived[...].reshape(patches * size, columns)
+            mine = pl.ds(pl.multiple_of(part * rows, rows), rows)
+            total[mine, :] = jnp.dot(high[mine, :], flat, preferred_element_type=jnp.float32)
+            return carry
+
+        lax.fori_loop(0, 2, half, 0)
+        fresh = total[...]
+        flat = arrived[...].reshape(patches * size, columns)
+        for k, copy in enumerate(copies):
+            copy.wait()
+            part = flat[k * depth : (k + 1) * depth]
+            fresh = fresh + jnp.dot(low[k], part, preferred_element_type=jnp.float32)
+        finish(fresh)
 
 
 def first_kernel(keeps, incident_hbm, own, received, inverse_hbm, current, incident, inverse, sems):
@@ -174,21 +188,24 @@
         staged[...] = field[...]
 
 
-def solve_kernel(high, low_hbm, arrived, staged, inverse, current, low, sems):
-    @pl.when(lax.axis_index("lag") == 0)
-    def _():
-        current[...] = solved(staged[...] - product(high, low_hbm, arrived, low, sems), inverse)
-
-
-def partial_kernel(high, low_hbm, arrived, staged, after, partial, low, sems):
+def solve_kernel(high, low_hbm, arrived, staged, inverse, current, low, total, sems):
+    def finish(fresh):
+        current[...] = solved(staged[...] - fresh, inverse)
+
+    product(lax.axis_index("lag") == 0, high, low_hbm, arrived, low, total, sems, finish)
+
+
+def partial_kernel(high, low_hbm, arrived, staged, after, partial, low, total, sems):
     del after
 
-    @pl.when(lax.axis_index("lag") > 0)
-    def _():
-        partial[...] = staged[...] + product(high, low_hbm, arrived, low, sems)
-
-
-def asked_kernel(table, asked, copy_of, sem):
+    def finish(fresh):
+        partial[...] = staged[...] + fresh
+
+    product(lax.axis_index("lag") > 0, high, low_hbm, arrived, low, total, sems, finish)
+
+
+def asked_kernel(table, after, asked, copy_of, sem):
+    del after
     started((table, copy_of, sem))[0].wait()
     for q in range(table.shape[0]):
         asked[q] = jnp.maximum(copy_of[q, 0, 0], 0)
@@ -273,21 +290,16 @@
 
     wanted, first_field = call(
         lambda *refs: request_kernel(per_patch, *refs),
-        [(HBM, (patches, 1, 128), jnp.int32), (VMEM, column, f32)],
+        [(HBM, (patches, 8, 128), jnp.int32), (VMEM, column, f32)],
         [(HBM, block_sources), (HBM, owner_map), (HBM, pending[0])],
         [
-            pltpu.VMEM((patches, 1, 128), jnp.int32),
+            pltpu.VMEM((patches, 8, 128), jnp.int32),
             pltpu.SMEM(block_sources.shape, jnp.int32),
             pltpu.SMEM(owner_map.shape, jnp.int32),
             DMA((3,)),
         ],
     )
-    asked = call(
-        asked_kernel,
-        [(SMEM, (patches,), jnp.int32)],
-        [(VMEM, exchange(wanted))],
-        [pltpu.SMEM(wanted.shape, jnp.int32), DMA],
-    )
+    requests = exchange(wanted)
     own, received, keeps = spread(first_field)
     solve_scratch = [pltpu.VMEM(column, bf16), pltpu.VMEM(self_inverse.shape, f32), DMA((3,))]
     current = call(
@@ -296,6 +308,12 @@
         [(HBM, incident), (VMEM, own), (VMEM, received), (HBM, self_inverse)],
         solve_scratch,
         solve_flops,
+    )
+    asked = call(
+        asked_kernel,
+        [(SMEM, (patches,), jnp.int32)],
+        [(VMEM, requests), (VMEM, current)],
+        [pltpu.SMEM(wanted.shape, jnp.int32), DMA],
     )
     chunk = max(n for n in range(1, 9) if listed % n == 0)
     panel = (unknowns, patches * size)
@@ -335,7 +353,7 @@
                 [pltpu.VMEM(column, bf16), DMA],
             )
             shared = [(VMEM, high), (HBM, low), (VMEM, arrived), (VMEM, staged)]
-            scratch = [pltpu.VMEM(low_panel, bf16), DMA((pieces,))]
+            scratch = [pltpu.VMEM(low_panel, bf16), pltpu.VMEM(column, f32), DMA((pieces,))]
             sizes = [all_flops, panel_bytes + arrived_bytes, panel_bytes + arrived_bytes]
             current = call(
                 solve_kernel, [(VMEM, column, bf16)], [*shared, (VMEM, inverse)], scratch, *sizes

time: 125 us -> 125 us (level)
  blocking collectives: 12.3 us -> 0 us
  starting transfers between devices: 31.4 us -> 38.8 us
  waiting for transfers between devices: 50 us -> 55.8 us
  Pallas kernels: 29.1 us -> 27.5 us
    all_to_all x1 -> x0, blocking collectives: 12.3 us -> none  [exchange(): return lax.all_to_all(x, 'patch', split_axis=0, concat_axis=0, tiled=True)]
    all_to_all x4 -> x5, starting transfers between devices: 16.7 us -> 22.6 us  [exchange(): return lax.all_to_all(x, 'patch', split_axis=0, concat_axis=0, tiled=True)]
    all_to_all x4 -> x5, waiting for transfers between devices: 10.3 us -> 15.7 us  [exchange(): return lax.all_to_all(x, 'patch', split_axis=0, concat_axis=0, tiled=True)]
    pallas_call x21, Pallas kernels: 29.1 us -> 27.5 us  [call(): run(*(pltpu.with_memory_space_constraint(x, space) for space, x in ins))]
    ppermute x4, starting transfers between devices: 9.58 us -> 11 us  [spread(): received = lax.ppermute(x, 'lag', pairs)]
  transfers between devices with their start and end apart: 12 -> 13, of which waited for: 11 -> 12; matrix products, arithmetic and copies ran while one was open for 0% -> 0% of each run, Pallas kernels for 10% -> 10%
where the time goes in v4:
time: 125 us; the launch traced here: 123 us
  waiting for transfers between devices  55.8 us (45%)
  starting transfers between devices  38.8 us (31%)
  Pallas kernels  27.5 us (22%)
    ppermute x4, waiting for transfers between devices, shifted(): return lax.ppermute(x, 'lag', [(i, i - 1) for i in range(1, sections)])  34.3 us
    pallas_call x21, Pallas kernels, call(): run(*(pltpu.with_memory_space_constraint(x, space) for space, x in ins))  27.5 us
    all_to_all x5, starting transfers between devices, exchange(): return lax.all_to_all(x, 'patch', split_axis=0, concat_axis=0, tiled=True)  22.6 us
    all_to_all x5, waiting for transfers between devices, exchange(): return lax.all_to_all(x, 'patch', split_axis=0, concat_axis=0, tiled=True)  15.7 us
    ppermute x4, starting transfers between devices, spread(): received = lax.ppermute(x, 'lag', pairs)  11 us
    ppermute x4, waiting for transfers between devices, spread(): received = lax.ppermute(x, 'lag', pairs)  5.82 us
    ppermute x4, starting transfers between devices, shifted(): return lax.ppermute(x, 'lag', [(i, i - 1) for i in range(1, sections)])  5.17 us
  transfers between devices with their start and end apart: 13, of which 12 were waited for; matrix products, arithmetic and copies ran while one was open for 0% of the time, Pallas kernels for 10%

profile of v4, /device:TPU:0, one launch (start us, length us, event | category | flops | bytes accessed | tf_op | source)
XLA Modules:
  0.0 123.1 jit_solution(2796648954726315093)
XLA Ops:
  0.6 2.0 %shard_map.86 = (s32[16,8,128]{2,1,0:T(8,128)}, f32[512,128]{1,0:T(8,128)S(1)}) custom-call(s32[1,1,56]{2,1,0:T(1,128)} %refs_1_.3, s32[64]{0:T(128)} %refs_2_.1, f32[512,128]{1,0:T(8,128)} %bitcast.3), custom_call_target="tpu_custom_call" | custom-call | tf_op jit(solution)/shard_map/pallas_call | solution.py:26
  2.6 4.9 %collective-permute-start = (f32[512,128]{1,0:T(8,128)S(1)}, f32[512,128]{1,0:T(8,128)S(1)}, u32[]{:S(2)}, u32[]{:S(2)}) collective-permute-start(f32[512,128]{1,0:T(8,128)S(1)} %get-tuple-element.22.refs_1_), channel_id=1, source_target_pairs={{0,16},{1,17},{2,18},{3,19},{4,20},{5,21},{6,22},{7,23},{8,24},{9,... | collective-permute-start | bytes 786440 | tf_op jit(solution)/shard_map/ppermute | solution.py:257
  7.5 5.9 %all-to-all-start = ((s32[16,8,128]{2,1,0:T(8,128)}), s32[16,8,128]{2,1,0:T(8,128)S(1)}, u32[]{:S(2)}, u32[]{:S(2)}) async-start(s32[16,8,128]{2,1,0:T(8,128)} %get-tuple-element.21), calls=%async_computation | async-start | bytes 131072 | tf_op jit(solution)/shard_map/all_to_all | solution.py:275
  13.4 1.4 %shard_map.87.after.refs_1_ = bf16[512,128]{1,0:T(8,128)(2,1)S(1)} custom-call(bf16[4,512,128]{2,1,0:T(8,128)(2,1)} %refs_0_.11, f32[512,128]{1,0:T(8,128)S(1)} %get-tuple-element.22.refs_1_, f32[512,128]{1,0:T(8,128)S(1)} %collective-permute-done.refs_2_, f32[4,128,128]{2,1,0:T(8,128)} %refs_4_.1), custom_call_target="tpu_custom_call" | custom-call | flops 100663296 | tf_op jit(solution)/shard_map/pallas_call | solution.py:26
  14.9 5.4 %all-to-all-done.table = s32[16,8,128]{2,1,0:T(8,128)S(1)} async-done(((s32[16,8,128]{2,1,0:T(8,128)}), s32[16,8,128]{2,1,0:T(8,128)S(1)}, u32[]{:S(2)}, u32[]{:S(2)}) %all-to-all-start) | async-done | bytes 65568 | tf_op jit(solution)/shard_map/all_to_all | solution.py:275
  20.3 1.6 %shard_map.88.refs_0_ = s32[16]{0:T(128)S(4)} custom-call(s32[16,8,128]{2,1,0:T(8,128)S(1)} %all-to-all-done.table, bf16[512,128]{1,0:T(8,128)(2,1)S(1)} %shard_map.87.after.refs_1_), custom_call_target="tpu_custom_call" | custom-call | tf_op jit(solution)/shard_map/pallas_call | solution.py:26
  23.0 3.6 %all-to-all-start.1 = ((bf16[16,128,128]{2,1,0:T(8,128)(2,1)}), bf16[16,128,128]{2,1,0:T(8,128)(2,1)S(1)}, u32[]{:S(2)}, u32[]{:S(2)}) async-start(bf16[16,128,128]{2,1,0:T(8,128)(2,1)} %get-tuple-element.25), calls=%async_computation.1 | async-start | bytes 1048576 | tf_op jit(solution)/shard_map/all_to_all | solution.py:275
  26.6 1.3 %collective-permute-start.1 = (f32[512,128]{1,0:T(8,128)S(1)}, f32[512,128]{1,0:T(8,128)S(1)}, u32[]{:S(2)}, u32[]{:S(2)}) collective-permute-start(f32[512,128]{1,0:T(8,128)S(1)} %bitcast.4), channel_id=1, source_target_pairs={{16,0},{17,1},{18,2},{19,3},{20,4},{21,5},{22,6},{23,7},{24,8},{25... | collective-permute-start | bytes 786440 | tf_op jit(solution)/shard_map/ppermute | solution.py:246
  27.9 5.2 %shard_map.89 = (bf16[512,2048]{1,0:T(8,128)(2,1)S(1)}, bf16[4,512,512]{2,1,0:T(8,128)(2,1)}, f32[4,128,128]{2,1,0:T(8,128)S(1)}) custom-call(s32[1,1,56]{2,1,0:T(1,128)} %refs_0_.8, s32[1,1,56]{2,1,0:T(1,128)} %refs_1_.3, s32[64]{0:T(128)} %refs_2_.1, f32[1,1,56,128,128]{4,3,2,1,0:T(8,128)} %refs_3_.3, f32[4,128,128]{2,1,0:T(8,128)} %refs_4_.1), custom_call_target="tpu_custom_call" | custom-call | bytes 7864320 | tf_op jit(solution)/shard_map/pallas_call | solution.py:26
  33.1 3.9 %collective-permute-done.1.refs_1_ = f32[512,128]{1,0:T(8,128)S(1)} collective-permute-done((f32[512,128]{1,0:T(8,128)S(1)}, f32[512,128]{1,0:T(8,128)S(1)}, u32[]{:S(2)}, u32[]{:S(2)}) %collective-permute-start.1) | collective-permute-done | bytes 262176 | tf_op jit(solution)/shard_map/ppermute | solution.py:246
  37.9 3.1 %all-to-all-done.1.arrived = bf16[16,128,128]{2,1,0:T(8,128)(2,1)S(1)} async-done(((bf16[16,128,128]{2,1,0:T(8,128)(2,1)}), bf16[16,128,128]{2,1,0:T(8,128)(2,1)S(1)}, u32[]{:S(2)}, u32[]{:S(2)}) %all-to-all-start.1) | async-done | bytes 524320 | tf_op jit(solution)/shard_map/all_to_all | solution.py:275
  41.0 2.8 %shard_map.92.after.refs_1_ = bf16[512,128]{1,0:T(8,128)(2,1)S(1)} custom-call(bf16[512,2048]{1,0:T(8,128)(2,1)S(1)} %get-tuple-element.23.high, bf16[4,512,512]{2,1,0:T(8,128)(2,1)} %get-tuple-element.24.low_hbm, bf16[16,128,128]{2,1,0:T(8,128)(2,1)S(1)} %all-to-all-done.1.arrived, f32[512,128]{1,0:T(8,128)S(1)} %shard_map.91.staged, ...), custom_call_target="tpu_custom_call" | custom-call | flops 536870912 | bytes 4718592 | tf_op jit(solution)/shard_map/pallas_call | solution.py:26
  43.8 1.3 %collective-permute-start.2 = (bf16[512,128]{1,0:T(8,128)(2,1)S(1)}, bf16[512,128]{1,0:T(8,128)(2,1)S(1)}, u32[]{:S(2)}, u32[]{:S(2)}) collective-permute-start(bf16[512,128]{1,0:T(8,128)(2,1)S(1)} %shard_map.92.after.refs_1_), channel_id=1, source_target_pairs={{0,16},{1,17},{2,18},{3,19},{4,20},{5,21},{6,22},{7,23},{8,24},{9,... | collective-permute-start | bytes 393224 | tf_op jit(solution)/shard_map/ppermute | solution.py:257
  46.2 2.1 %collective-permute-done.2.refs_1_ = bf16[512,128]{1,0:T(8,128)(2,1)S(1)} collective-permute-done((bf16[512,128]{1,0:T(8,128)(2,1)S(1)}, bf16[512,128]{1,0:T(8,128)(2,1)S(1)}, u32[]{:S(2)}, u32[]{:S(2)}) %collective-permute-start.2) | collective-permute-done | bytes 131104 | tf_op jit(solution)/shard_map/ppermute | solution.py:257
  48.5 4.3 %all-to-all-start.2 = ((bf16[16,128,128]{2,1,0:T(8,128)(2,1)}), bf16[16,128,128]{2,1,0:T(8,128)(2,1)S(1)}, u32[]{:S(2)}, u32[]{:S(2)}) async-start(bf16[16,128,128]{2,1,0:T(8,128)(2,1)} %get-tuple-element.30), calls=%async_computation.2 | async-start | bytes 1048576 | tf_op jit(solution)/shard_map/all_to_all | solution.py:275
  52.8 1.3 %collective-permute-start.3 = (f32[512,128]{1,0:T(8,128)S(1)}, f32[512,128]{1,0:T(8,128)S(1)}, u32[]{:S(2)}, u32[]{:S(2)}) collective-permute-start(f32[512,128]{1,0:T(8,128)S(1)} %shard_map.93.refs_2_), channel_id=1, source_target_pairs={{16,0},{17,1},{18,2},{19,3},{20,4},{21,5},{22,6},{23,7},{24,8},{25... | collective-permute-start | bytes 786440 | tf_op jit(solution)/shard_map/ppermute | solution.py:246
  54.1 10.1 %collective-permute-done.3.refs_1_ = f32[512,128]{1,0:T(8,128)S(1)} collective-permute-done((f32[512,128]{1,0:T(8,128)S(1)}, f32[512,128]{1,0:T(8,128)S(1)}, u32[]{:S(2)}, u32[]{:S(2)}) %collective-permute-start.3) | collective-permute-done | bytes 262176 | tf_op jit(solution)/shard_map/ppermute | solution.py:246
  65.2 2.1 %all-to-all-done.2.arrived = bf16[16,128,128]{2,1,0:T(8,128)(2,1)S(1)} async-done(((bf16[16,128,128]{2,1,0:T(8,128)(2,1)}), bf16[16,128,128]{2,1,0:T(8,128)(2,1)S(1)}, u32[]{:S(2)}, u32[]{:S(2)}) %all-to-all-start.2) | async-done | bytes 524320 | tf_op jit(solution)/shard_map/all_to_all | solution.py:275
  67.3 2.8 %shard_map.97.after.refs_1_ = bf16[512,128]{1,0:T(8,128)(2,1)S(1)} custom-call(bf16[512,2048]{1,0:T(8,128)(2,1)S(1)} %get-tuple-element.23.high, bf16[4,512,512]{2,1,0:T(8,128)(2,1)} %get-tuple-element.24.low_hbm, bf16[16,128,128]{2,1,0:T(8,128)(2,1)S(1)} %all-to-all-done.2.arrived, f32[512,128]{1,0:T(8,128)S(1)} %shard_map.96.staged, ...), custom_call_target="tpu_custom_call" | custom-call | flops 536870912 | bytes 4718592 | tf_op jit(solution)/shard_map/pallas_call | solution.py:26
  70.1 2.4 %collective-permute-start.4 = (bf16[512,128]{1,0:T(8,128)(2,1)S(1)}, bf16[512,128]{1,0:T(8,128)(2,1)S(1)}, u32[]{:S(2)}, u32[]{:S(2)}) collective-permute-start(bf16[512,128]{1,0:T(8,128)(2,1)S(1)} %shard_map.97.after.refs_1_), channel_id=1, source_target_pairs={{0,16},{1,17},{2,18},{3,19},{4,20},{5,21},{6,22},{7,23},{8,24},{9,... | collective-permute-start | bytes 393224 | tf_op jit(solution)/shard_map/ppermute | solution.py:257
  73.6 1.8 %collective-permute-done.4.refs_1_ = bf16[512,128]{1,0:T(8,128)(2,1)S(1)} collective-permute-done((bf16[512,128]{1,0:T(8,128)(2,1)S(1)}, bf16[512,128]{1,0:T(8,128)(2,1)S(1)}, u32[]{:S(2)}, u32[]{:S(2)}) %collective-permute-start.4) | collective-permute-done | bytes 131104 | tf_op jit(solution)/shard_map/ppermute | solution.py:257
  75.6 4.4 %all-to-all-start.3 = ((bf16[16,128,128]{2,1,0:T(8,128)(2,1)}), bf16[16,128,128]{2,1,0:T(8,128)(2,1)S(1)}, u32[]{:S(2)}, u32[]{:S(2)}) async-start(bf16[16,128,128]{2,1,0:T(8,128)(2,1)} %get-tuple-element.34), calls=%async_computation.3 | async-start | bytes 1048576 | tf_op jit(solution)/shard_map/all_to_all | solution.py:275
  81.3 10.1 %collective-permute-done.5.refs_1_ = f32[512,128]{1,0:T(8,128)S(1)} collective-permute-done((f32[512,128]{1,0:T(8,128)S(1)}, f32[512,128]{1,0:T(8,128)S(1)}, u32[]{:S(2)}, u32[]{:S(2)}) %collective-permute-start.5) | collective-permute-done | bytes 262176 | tf_op jit(solution)/shard_map/ppermute | solution.py:246
  92.4 2.1 %all-to-all-done.3.arrived = bf16[16,128,128]{2,1,0:T(8,128)(2,1)S(1)} async-done(((bf16[16,128,128]{2,1,0:T(8,128)(2,1)}), bf16[16,128,128]{2,1,0:T(8,128)(2,1)S(1)}, u32[]{:S(2)}, u32[]{:S(2)}) %all-to-all-start.3) | async-done | bytes 524320 | tf_op jit(solution)/shard_map/all_to_all | solution.py:275
  94.5 2.8 %shard_map.102.after.refs_1_ = bf16[512,128]{1,0:T(8,128)(2,1)S(1)} custom-call(bf16[512,2048]{1,0:T(8,128)(2,1)S(1)} %get-tuple-element.23.high, bf16[4,512,512]{2,1,0:T(8,128)(2,1)} %get-tuple-element.24.low_hbm, bf16[16,128,128]{2,1,0:T(8,128)(2,1)S(1)} %all-to-all-done.3.arrived, f32[512,128]{1,0:T(8,128)S(1)} %shard_map.101.staged, ...), custom_call_target="tpu_custom_call" | custom-call | flops 536870912 | bytes 4718592 | tf_op jit(solution)/shard_map/pallas_call | solution.py:26
  97.3 2.4 %collective-permute-start.6 = (bf16[512,128]{1,0:T(8,128)(2,1)S(1)}, bf16[512,128]{1,0:T(8,128)(2,1)S(1)}, u32[]{:S(2)}, u32[]{:S(2)}) collective-permute-start(bf16[512,128]{1,0:T(8,128)(2,1)S(1)} %shard_map.102.after.refs_1_), channel_id=1, source_target_pairs={{0,16},{1,17},{2,18},{3,19},{4,20},{5,21},{6,22},{7,23},{8,24},{9,... | collective-permute-start | bytes 393224 | tf_op jit(solution)/shard_map/ppermute | solution.py:257
  100.8 1.8 %collective-permute-done.6.refs_1_ = bf16[512,128]{1,0:T(8,128)(2,1)S(1)} collective-permute-done((bf16[512,128]{1,0:T(8,128)(2,1)S(1)}, bf16[512,128]{1,0:T(8,128)(2,1)S(1)}, u32[]{:S(2)}, u32[]{:S(2)}) %collective-permute-start.6) | collective-permute-done | bytes 131104 | tf_op jit(solution)/shard_map/ppermute | solution.py:257
  102.8 4.4 %all-to-all-start.4 = ((bf16[16,128,128]{2,1,0:T(8,128)(2,1)}), bf16[16,128,128]{2,1,0:T(8,128)(2,1)S(1)}, u32[]{:S(2)}, u32[]{:S(2)}) async-start(bf16[16,128,128]{2,1,0:T(8,128)(2,1)} %get-tuple-element.39), calls=%async_computation.4 | async-start | bytes 1048576 | tf_op jit(solution)/shard_map/all_to_all | solution.py:275
  107.2 1.3 %collective-permute-start.7 = (f32[512,128]{1,0:T(8,128)S(1)}, f32[512,128]{1,0:T(8,128)S(1)}, u32[]{:S(2)}, u32[]{:S(2)}) collective-permute-start(f32[512,128]{1,0:T(8,128)S(1)} %shard_map.103.refs_2_), channel_id=1, source_target_pairs={{16,0},{17,1},{18,2},{19,3},{20,4},{21,5},{22,6},{23,7},{24,8},{25... | collective-permute-start | bytes 786440 | tf_op jit(solution)/shard_map/ppermute | solution.py:246
  108.5 10.1 %collective-permute-done.7.field = f32[512,128]{1,0:T(8,128)S(1)} collective-permute-done((f32[512,128]{1,0:T(8,128)S(1)}, f32[512,128]{1,0:T(8,128)S(1)}, u32[]{:S(2)}, u32[]{:S(2)}) %collective-permute-start.7) | collective-permute-done | bytes 262176 | tf_op jit(solution)/shard_map/ppermute | solution.py:246
  118.7 3.0 %all-to-all-done.4.arrived = bf16[16,128,128]{2,1,0:T(8,128)(2,1)S(1)} async-done(((bf16[16,128,128]{2,1,0:T(8,128)(2,1)}), bf16[16,128,128]{2,1,0:T(8,128)(2,1)S(1)}, u32[]{:S(2)}, u32[]{:S(2)}) %all-to-all-start.4) | async-done | bytes 524320 | tf_op jit(solution)/shard_map/all_to_all | solution.py:275
  121.7 1.4 %shard_map.106 = f32[512,128]{1,0:T(8,128)} custom-call(bf16[512,2048]{1,0:T(8,128)(2,1)S(1)} %get-tuple-element.23.high, bf16[16,128,128]{2,1,0:T(8,128)(2,1)S(1)} %all-to-all-done.4.arrived, f32[512,128]{1,0:T(8,128)S(1)} %collective-permute-done.7.field), custom_call_target="tpu_custom_call" | custom-call | flops 536870912 | bytes 4718592 | tf_op jit(solution)/shard_map/pallas_call | solution.py:26
  (17 shorter events, 8.7 us)
Async XLA Ops:
  0.6 25.9 %copy-start = (f32[1,512,128]{2,1,0:T(8,128)S(1)}, f32[1,512,128]{2,1,0:T(8,128)}, u32[]{:S(2)}) copy-start(f32[1,512,128]{2,1,0:T(8,128)} %param.8) | copy-start | bytes 786436
  2.6 10.8 %collective-permute-start = (f32[512,128]{1,0:T(8,128)S(1)}, f32[512,128]{1,0:T(8,128)S(1)}, u32[]{:S(2)}, u32[]{:S(2)}) collective-permute-start(f32[512,128]{1,0:T(8,128)S(1)} %get-tuple-element.22.refs_1_), channel_id=1, source_target_pairs={{0,16},{1,17},{2,18},{3,19},{4,20},{5,21},{6,22},{7,23},{8,24},{9,... | collective-permute-start | bytes 786440 | tf_op jit(solution)/shard_map/ppermute | solution.py:257
  7.5 12.8 %all-to-all-start = ((s32[16,8,128]{2,1,0:T(8,128)}), s32[16,8,128]{2,1,0:T(8,128)S(1)}, u32[]{:S(2)}, u32[]{:S(2)}) async-start(s32[16,8,128]{2,1,0:T(8,128)} %get-tuple-element.21), calls=%async_computation | async-start | bytes 131072 | tf_op jit(solution)/shard_map/all_to_all | solution.py:275
  23.0 18.0 %all-to-all-start.1 = ((bf16[16,128,128]{2,1,0:T(8,128)(2,1)}), bf16[16,128,128]{2,1,0:T(8,128)(2,1)S(1)}, u32[]{:S(2)}, u32[]{:S(2)}) async-start(bf16[16,128,128]{2,1,0:T(8,128)(2,1)} %get-tuple-element.25), calls=%async_computation.1 | async-start | bytes 1048576 | tf_op jit(solution)/shard_map/all_to_all | solution.py:275
  26.6 10.4 %collective-permute-start.1 = (f32[512,128]{1,0:T(8,128)S(1)}, f32[512,128]{1,0:T(8,128)S(1)}, u32[]{:S(2)}, u32[]{:S(2)}) collective-permute-start(f32[512,128]{1,0:T(8,128)S(1)} %bitcast.4), channel_id=1, source_target_pairs={{16,0},{17,1},{18,2},{19,3},{20,4},{21,5},{22,6},{23,7},{24,8},{25... | collective-permute-start | bytes 786440 | tf_op jit(solution)/shard_map/ppermute | solution.py:246
  43.8 4.5 %collective-permute-start.2 = (bf16[512,128]{1,0:T(8,128)(2,1)S(1)}, bf16[512,128]{1,0:T(8,128)(2,1)S(1)}, u32[]{:S(2)}, u32[]{:S(2)}) collective-permute-start(bf16[512,128]{1,0:T(8,128)(2,1)S(1)} %shard_map.92.after.refs_1_), channel_id=1, source_target_pairs={{0,16},{1,17},{2,18},{3,19},{4,20},{5,21},{6,22},{7,23},{8,24},{9,... | collective-permute-start | bytes 393224 | tf_op jit(solution)/shard_map/ppermute | solution.py:257
  48.5 18.8 %all-to-all-start.2 = ((bf16[16,128,128]{2,1,0:T(8,128)(2,1)}), bf16[16,128,128]{2,1,0:T(8,128)(2,1)S(1)}, u32[]{:S(2)}, u32[]{:S(2)}) async-start(bf16[16,128,128]{2,1,0:T(8,128)(2,1)} %get-tuple-element.30), calls=%async_computation.2 | async-start | bytes 1048576 | tf_op jit(solution)/shard_map/all_to_all | solution.py:275
  52.8 11.4 %collective-permute-start.3 = (f32[512,128]{1,0:T(8,128)S(1)}, f32[512,128]{1,0:T(8,128)S(1)}, u32[]{:S(2)}, u32[]{:S(2)}) collective-permute-start(f32[512,128]{1,0:T(8,128)S(1)} %shard_map.93.refs_2_), channel_id=1, source_target_pairs={{16,0},{17,1},{18,2},{19,3},{20,4},{21,5},{22,6},{23,7},{24,8},{25... | collective-permute-start | bytes 786440 | tf_op jit(solution)/shard_map/ppermute | solution.py:246
  70.1 5.3 %collective-permute-start.4 = (bf16[512,128]{1,0:T(8,128)(2,1)S(1)}, bf16[512,128]{1,0:T(8,128)(2,1)S(1)}, u32[]{:S(2)}, u32[]{:S(2)}) collective-permute-start(bf16[512,128]{1,0:T(8,128)(2,1)S(1)} %shard_map.97.after.refs_1_), channel_id=1, source_target_pairs={{0,16},{1,17},{2,18},{3,19},{4,20},{5,21},{6,22},{7,23},{8,24},{9,... | collective-permute-start | bytes 393224 | tf_op jit(solution)/shard_map/ppermute | solution.py:257
  75.6 18.9 %all-to-all-start.3 = ((bf16[16,128,128]{2,1,0:T(8,128)(2,1)}), bf16[16,128,128]{2,1,0:T(8,128)(2,1)S(1)}, u32[]{:S(2)}, u32[]{:S(2)}) async-start(bf16[16,128,128]{2,1,0:T(8,128)(2,1)} %get-tuple-element.34), calls=%async_computation.3 | async-start | bytes 1048576 | tf_op jit(solution)/shard_map/all_to_all | solution.py:275
  80.0 11.4 %collective-permute-start.5 = (f32[512,128]{1,0:T(8,128)S(1)}, f32[512,128]{1,0:T(8,128)S(1)}, u32[]{:S(2)}, u32[]{:S(2)}) collective-permute-start(f32[512,128]{1,0:T(8,128)S(1)} %shard_map.98.refs_2_), channel_id=1, source_target_pairs={{16,0},{17,1},{18,2},{19,3},{20,4},{21,5},{22,6},{23,7},{24,8},{25... | collective-permute-start | bytes 786440 | tf_op jit(solution)/shard_map/ppermute | solution.py:246
  97.3 5.3 %collective-permute-start.6 = (bf16[512,128]{1,0:T(8,128)(2,1)S(1)}, bf16[512,128]{1,0:T(8,128)(2,1)S(1)}, u32[]{:S(2)}, u32[]{:S(2)}) collective-permute-start(bf16[512,128]{1,0:T(8,128)(2,1)S(1)} %shard_map.102.after.refs_1_), channel_id=1, source_target_pairs={{0,16},{1,17},{2,18},{3,19},{4,20},{5,21},{6,22},{7,23},{8,24},{9,... | collective-permute-start | bytes 393224 | tf_op jit(solution)/shard_map/ppermute | solution.py:257
  102.8 18.9 %all-to-all-start.4 = ((bf16[16,128,128]{2,1,0:T(8,128)(2,1)}), bf16[16,128,128]{2,1,0:T(8,128)(2,1)S(1)}, u32[]{:S(2)}, u32[]{:S(2)}) async-start(bf16[16,128,128]{2,1,0:T(8,128)(2,1)} %get-tuple-element.39), calls=%async_computation.4 | async-start | bytes 1048576 | tf_op jit(solution)/shard_map/all_to_all | solution.py:275
  107.2 11.4 %collective-permute-start.7 = (f32[512,128]{1,0:T(8,128)S(1)}, f32[512,128]{1,0:T(8,128)S(1)}, u32[]{:S(2)}, u32[]{:S(2)}) collective-permute-start(f32[512,128]{1,0:T(8,128)S(1)} %shard_map.103.refs_2_), channel_id=1, source_target_pairs={{16,0},{17,1},{18,2},{19,3},{20,4},{21,5},{22,6},{23,7},{24,8},{25... | collective-permute-start | bytes 786440 | tf_op jit(solution)/shard_map/ppermute | solution.py:246
